TPU v7x, 256 devices: a whole 4x4x8 slice. The times are simulated.
256 devices in a mesh: ctx: 32 (over x_hi, z, core), head: 8 (over x_lo, y).
Axes of the slice: x: 4 (x_hi: 2, x_lo: 2; x = x_hi * 2 + x_lo), y: 4, z: 8, core: 2. Of those that a mesh axis runs over, the one named last changes fastest.
Arguments:
- queries_one: bfloat16 [4096, 4096], P('ctx', 'head'), may hold values from -6 to 6
- grads_one: bfloat16 [4096, 4096], P('ctx', 'head'), may hold values from -6 to 6
- queries_two: bfloat16 [4096, 4096], P('ctx', 'head'), may hold values from -6 to 6
- grads_two: bfloat16 [4096, 4096], P('ctx', 'head'), may hold values from -6 to 6
- key_rows: bfloat16 [4096, 1024], P('ctx', 'head'), may hold values from -6 to 6
- value_rows: bfloat16 [4096, 1024], P('ctx', 'head'), may hold values from -6 to 6
- shared_input: bfloat16 [4096, 8192], P('ctx'), may hold values from -6 to 6
- key_weight: bfloat16 [8192, 1024], P(None, 'head'), may hold values from -0.09375 to 0.09375
- value_weight: bfloat16 [8192, 1024], P(None, 'head'), may hold values from -0.0625 to 0.0625
- block_order: int32 [64], replicated, may hold values from 0 to 63, as said below
Outputs:
- query_grad_one: bfloat16 [4096, 4096], P('ctx', 'head')
- query_grad_two: bfloat16 [4096, 4096], P('ctx', 'head')
- input_grad: bfloat16 [4096, 8192], P('ctx', 'head')
- key_weight_grad: float32 [8192, 1024], P('ctx', 'head')
- value_weight_grad: float32 [8192, 1024], P('ctx', 'head')
Inputs may be any that keep to these rules, and one draw needn't show every extreme that they name: `block_order`: each block 0 to 63 once; slots 2c and 2c + 1 hold blocks i and 63 - i for some i.
All inputs are finite; a program needn't handle non-finite values.
Results may differ from a plain program's by a relative error of at most 0.013.
Values may be sent and summed in bfloat16 or wider, within the bound.
No kernel may reach another device: no remote copies, remote signals or barrier semaphores. Data moves between devices by JAX's collectives and lax.ppermute only.
A program may use at most 128 MiB of HBM per device.

v0:
```python
import functools
import math

import jax
import jax.numpy as jnp
from jax import lax
from jax.experimental import pallas as pl
from jax.experimental.pallas import tpu as pltpu
from jax.sharding import Mesh
from jax.sharding import PartitionSpec as P

H = 32
KV = 8
DH = 128
GROUP = H // KV
CTX = ("xh", "z", "core")
HEAD = ("xl", "y")
NT = (((1,), (1,)), ((), ()))
TN = (((0,), (0,)), ((), ()))
f32 = jnp.float32
bf16 = jnp.bfloat16
SCALE = 1.0 / math.sqrt(DH)
TO_LOG2 = SCALE * math.log2(math.e)
LOWEST = -1e30
BIG = 56 * 2**20
MIDDLE = 16 * 2**20
SMALL = 8 * 2**20
VMEM = pl.BlockSpec(memory_space=pltpu.VMEM)
SMEM = pl.BlockSpec(memory_space=pltpu.SMEM)
ANY = pl.BlockSpec(memory_space=pl.ANY)


class Plan:
    def __init__(self, order, where, n_keys, half):
        self.half = half
        self.n_keys = n_keys
        self.order, self.where = order, where
        self.near = []
        for b in range(n_keys):
            slot = where[4 + b]
            self.near.append(jnp.minimum(order[slot], order[slot + 1]))
        self.rank = []
        for b in range(n_keys):
            r = jnp.int32(0)
            for o in range(n_keys):
                r += jnp.where(self.near[o] < self.near[b], 1, 0)
            self.rank.append(r)

    def key_rows(self, b, i):
        pos = self.order[self.where[4 + b] + i]
        r = self.rank[b]
        at = jnp.where(pos == self.near[b], r, 2 * self.n_keys - 1 - r)
        return pl.ds(pl.multiple_of(at * self.half, self.half), self.half)

    def limits(self, a, width):
        slot = self.where[a]
        first, second = self.order[slot], self.order[slot + 1]
        mine = jnp.minimum(first, second)
        below, upto = jnp.int32(0), jnp.int32(0)
        for near in self.near:
            below += jnp.where(near < mine, 1, 0)
            upto += jnp.where(near <= mine, 1, 0)
        early, late = upto, 2 * self.n_keys - below
        inside = lax.rem(lax.broadcasted_iota(jnp.int32, (1, width), 1), self.half)
        same = upto > below

        def last(blocks):
            return jnp.where(same, (blocks - 1) * self.half + inside, blocks * self.half - 1)

        return early, late, last(early), last(late)


def load_heads(a, ref, q_all, g_all, order, where, half):
    slot = where[a]
    late_at = jnp.where(order[slot] > order[slot + 1], 0, 1)
    for part, at in ((0, late_at), (1, 1 - late_at)):
        rows = pl.ds(pl.multiple_of(at * half, half), half)
        for layer in range(2):
            for h in range(GROUP):
                r = (layer * GROUP + h) * half
                c = (layer * 2 * GROUP + h) * DH
                q_all[part, r:r + half, :] = ref[rows, c:c + DH]
                c += GROUP * DH
                g_all[part, r:r + half, :] = ref[rows, c:c + DH]


def fetch(pairs, sems):
    copies = [pltpu.make_async_copy(src, dst, sems.at[i]) for i, (src, dst) in enumerate(pairs)]
    for copy in copies:
        copy.start()
    return copies


def sort_keys(plan, kv, k_sorted, v_sorted):
    for b in range(plan.n_keys):
        for i in range(2):
            to = plan.key_rows(b, i)
            rows = slice(i * plan.half, (i + 1) * plan.half)
            k_sorted[to, :] = kv[b, rows, :DH]
            v_sorted[to, :] = kv[b, rows, DH:2 * DH]


def fold(x, op):
    return op(x.reshape(x.shape[0] // 8, 8, x.shape[1]), axis=0)


def tiles(seen, n_keys, half, part):
    step = n_keys * half // 2
    if part == 0:
        return (
            (0, 2 * step, None, False),
            (2 * step, step, seen > n_keys, True),
            (3 * step, step, seen > n_keys + n_keys // 2, True),
        )
    return ((0, step, seen > 0, True), (step, step, seen > n_keys // 2, True))


def under(condition, body):
    if condition is None:
        body()
    else:
        pl.when(condition)(body)


def masked_scores(k, q, start, last, masked):
    s = lax.dot_general(k, q, NT, preferred_element_type=f32)
    if masked:
        key = start + lax.broadcasted_iota(jnp.int32, s.shape, 0)
        s = jnp.where(key <= last, s, -jnp.inf)
    return s


def stats_kernel(
    order, where, own, far, side, both, packed, stats, held, kv_held, k_sorted, v_sorted, q_all, g_all, sems,
    scores, peak, total, delta,
):
    half = own.shape[0] // 2
    n_keys = packed.shape[0]
    width = q_all.shape[1]
    copies = fetch(
        [(packed, kv_held)] + [(ref, held.at[a]) for a, ref in enumerate((own, far, side, both))], sems
    )
    plan = Plan(order, where, n_keys, half)
    copies[0].wait()
    sort_keys(plan, kv_held, k_sorted, v_sorted)
    for a in range(4):
        copies[1 + a].wait()
        load_heads(a, held.at[a], q_all, g_all, order, where, half)
        early, late, last_early, last_late = plan.limits(a, width)
        for part, seen, last in ((0, late, last_late), (1, early, last_early)):
            q, g = q_all[part], g_all[part]
            peak[...] = jnp.full(peak.shape, LOWEST, f32)
            for start, size, condition, masked in tiles(seen, n_keys, half, part):

                def score():
                    s = masked_scores(k_sorted[start:start + size, :], q, start, last, masked)
                    scores[start:start + size, :] = s
                    peak[...] = jnp.maximum(peak[...], fold(s, jnp.max))

                under(condition, score)
            top = jnp.max(peak[...], axis=0, keepdims=True) * TO_LOG2
            total[...] = jnp.zeros(total.shape, f32)
            delta[...] = jnp.zeros(delta.shape, f32)
            for start, size, condition, masked in tiles(seen, n_keys, half, part):

                def weigh():
                    e = jnp.exp2(scores[start:start + size, :] * TO_LOG2 - top)
                    d = lax.dot_general(
                        v_sorted[start:start + size, :], g, NT, preferred_element_type=f32
                    )
                    total[...] += fold(e, jnp.sum)
                    delta[...] += fold(e * d, jnp.sum)

                under(condition, weigh)
            row = 2 * a + part
            stats[0, row:row + 1, :] = top
            stats[1, row:row + 1, :] = jnp.sum(total[...], axis=0, keepdims=True)
            stats[2, row:row + 1, :] = jnp.sum(delta[...], axis=0, keepdims=True)


def grads_kernel(
    order, where, own, far, side, both, packed, s_own, s_far, s_side, s_both, dq_own, dq_far, dq_pair, dkv,
    held, kv_held, k_sorted, v_sorted, q_all, g_all, sems, s_held, out_mine, out_pair, out_kv, out_sems, dk, dv, dq,
):
    half = own.shape[0] // 2
    n_keys = packed.shape[0]
    width = q_all.shape[1]
    copies = fetch(
        [(packed, kv_held)]
        + [(ref, held.at[a]) for a, ref in enumerate((own, far, side, both))]
        + [(ref, s_held.at[a]) for a, ref in enumerate((s_own, s_far, s_side, s_both))],
        sems,
    )
    plan = Plan(order, where, n_keys, half)
    copies[0].wait()
    sort_keys(plan, kv_held, k_sorted, v_sorted)
    dk[...] = jnp.zeros(dk.shape, f32)
    dv[...] = jnp.zeros(dv.shape, f32)
    for copy in copies[5:9]:
        copy.wait()
    sent = []
    for a, out in enumerate((dq_own, dq_far, dq_pair.at[0], dq_pair.at[1])):
        dq_out = out_pair.at[a - 2] if a > 1 else out_mine.at[a]
        copies[1 + a].wait()
        load_heads(a, held.at[a], q_all, g_all, order, where, half)
        early, late, last_early, last_late = plan.limits(a, width)
        slot = where[a]
        late_at = jnp.where(order[slot] > order[slot + 1], 0, 1)
        for part, seen, last, at in ((0, late, last_late, late_at), (1, early, last_early, 1 - late_at)):
            q, g = q_all[part], g_all[part]
            shares = []
            for flip in range(4):
                r = 2 * (a ^ flip) + part
                shares.append(tuple(s_held[flip, j, r:r + 1, :] for j in range(3)))
            top = functools.reduce(jnp.maximum, (t for t, _, _ in shares))
            total = sum(n * jnp.exp2(t - top) for t, n, _ in shares)
            delta = sum(d * jnp.exp2(t - top) for t, _, d in shares) / total
            base = top + jnp.log2(total)
            dq[...] = jnp.zeros(dq.shape, f32)
            for start, size, condition, masked in tiles(seen, n_keys, half, part):

                def grads():
                    span = slice(start, start + size)
                    k = k_sorted[span, :]
                    s = masked_scores(k, q, start, last, masked)
                    p = jnp.exp2(s * TO_LOG2 - base)
                    d = lax.dot_general(v_sorted[span, :], g, NT, preferred_element_type=f32)
                    ds = (p * (d - delta)).astype(bf16)
                    dv[span, :] += jnp.dot(p.astype(bf16), g, preferred_element_type=f32)
                    dk[span, :] += jnp.dot(ds, q, preferred_element_type=f32)
                    dq[...] += lax.dot_general(k, ds, TN, preferred_element_type=f32)

                under(condition, grads)
            turned = (dq[...] * SCALE).T.astype(dq_out.dtype)
            rows = pl.ds(pl.multiple_of(at * half, half), half)
            for j in range(2 * GROUP):
                dq_out[rows, j * DH:(j + 1) * DH] = turned[j * half:(j + 1) * half, :]
        copy = pltpu.make_async_copy(dq_out, out, out_sems.at[a])
        copy.start()
        sent.append(copy)
    for b in range(n_keys):
        for i in range(2):
            of = plan.key_rows(b, i)
            rows = slice(i * half, (i + 1) * half)
            out_kv[b, rows, :DH] = (dk[of, :] * SCALE).astype(bf16)
            out_kv[b, rows, DH:] = dv[of, :].astype(bf16)
    copy = pltpu.make_async_copy(out_kv, dkv, out_sems.at[4])
    copy.start()
    for copy in sent + [copy]:
        copy.wait()


def scratch(n_keys, rows, copies):
    width = GROUP * rows
    return [
        pltpu.VMEM((4, rows, 4 * GROUP * DH), bf16),
        pltpu.VMEM((n_keys, rows, 2 * DH), bf16),
        pltpu.VMEM((n_keys * rows, DH), bf16),
        pltpu.VMEM((n_keys * rows, DH), bf16),
        pltpu.VMEM((2, width, DH), bf16),
        pltpu.VMEM((2, width, DH), bf16),
        pltpu.SemaphoreType.DMA((copies,)),
    ]


def cost(n_keys, rows, products):
    pairs = 4 * GROUP * rows * n_keys * rows
    return pl.CostEstimate(
        flops=2 * products * pairs * DH, bytes_accessed=8 * 2**20, transcendentals=pairs
    )


def attention_stats(order, where, own, far, side, both, packed):
    n_keys, rows, _ = packed.shape
    width = GROUP * rows
    return pl.pallas_call(
        stats_kernel,
        out_shape=jax.ShapeDtypeStruct((3, 8, width), f32),
        in_specs=[SMEM] * 2 + [ANY] * 5,
        out_specs=VMEM,
        scratch_shapes=scratch(n_keys, rows, 5)
        + [pltpu.VMEM((n_keys * rows, width), f32)]
        + [pltpu.VMEM((8, width), f32)] * 3,
        compiler_params=pltpu.CompilerParams(vmem_limit_bytes=BIG),
        cost_estimate=cost(n_keys, rows, 2),
    )(order, where, own, far, side, both, packed)


def attention_grads(order, where, own, far, side, both, packed, stats):
    n_keys, rows, _ = packed.shape
    width = GROUP * rows
    shape = (rows, 2 * GROUP * DH)
    return pl.pallas_call(
        grads_kernel,
        out_shape=(
            jax.ShapeDtypeStruct(shape, f32),
            jax.ShapeDtypeStruct(shape, f32),
            jax.ShapeDtypeStruct((2,) + shape, bf16),
            jax.ShapeDtypeStruct((n_keys, rows, 2 * DH), bf16),
        ),
        in_specs=[SMEM] * 2 + [ANY] * 9,
        out_specs=(ANY,) * 4,
        scratch_shapes=scratch(n_keys, rows, 9)
        + [
            pltpu.VMEM((4, 3, 8, width), f32),
            pltpu.VMEM((2,) + shape, f32),
            pltpu.VMEM((2,) + shape, bf16),
            pltpu.VMEM((n_keys, rows, 2 * DH), bf16),
            pltpu.SemaphoreType.DMA((5,)),
        ]
        + [pltpu.VMEM((n_keys * rows, DH), f32)] * 2
        + [pltpu.VMEM((DH, width), f32)],
        compiler_params=pltpu.CompilerParams(vmem_limit_bytes=BIG),
        cost_estimate=cost(n_keys, rows, 5),
    )(order, where, own, far, side, both, packed, *stats)


def pack_kernel(at, *refs):
    *heads, key_rows, value_rows, x, own, packed = refs[:-5]
    *cuts, sems = refs[-5:]
    count, _, wide = cuts[0].shape
    xh, core = at[0], at[1]
    pairs = []
    for j in range(count):
        for i, ref in enumerate((key_rows, value_rows)):
            pairs.append((ref, packed.at[j, :, i * DH:(i + 1) * DH]))
    side = heads[0].shape[1]
    for i, ref in enumerate(heads):
        pairs.append((ref, own.at[:, i * side:(i + 1) * side]))
    for i, cut in enumerate(cuts):
        lead = (xh ^ (i & 1)) * (2 * count) + (core ^ (i >> 1))
        for j in range(count):
            columns = pl.ds(pl.multiple_of((lead + 2 * j) * wide, wide), wide)
            pairs.append((x.at[:, columns], cut.at[j]))
    for copy in fetch(pairs, sems):
        copy.wait()


def pack(at, heads, key_rows, value_rows, x, count):
    rows = x.shape[0]
    cut = jax.ShapeDtypeStruct((count, rows, x.shape[1] // (4 * count)), bf16)
    return pl.pallas_call(
        pack_kernel,
        in_specs=[SMEM] + [ANY] * (len(heads) + 3),
        out_specs=(VMEM,) * 6,
        out_shape=(
            jax.ShapeDtypeStruct((rows, len(heads) * heads[0].shape[1]), bf16),
            jax.ShapeDtypeStruct((count, rows, 2 * DH), bf16),
            cut, cut, cut, cut,
        ),
        scratch_shapes=[pltpu.SemaphoreType.DMA((6 * count + len(heads),))],
        compiler_params=pltpu.CompilerParams(vmem_limit_bytes=BIG),
    )(at, *heads, key_rows, value_rows, x)


def key_sum_kernel(parts, grad):
    total = parts[0].astype(f32)
    for i in range(1, parts.shape[0]):
        total += parts[i].astype(f32)
    grad[...] = total.astype(bf16)


def key_sum(parts):
    return pl.pallas_call(
        key_sum_kernel,
        out_shape=jax.ShapeDtypeStruct(parts.shape[1:], bf16),
        in_specs=[VMEM],
        out_specs=VMEM,
        compiler_params=pltpu.CompilerParams(vmem_limit_bytes=SMALL),
    )(parts)


def input_terms_kernel(grad, key_weight, value_weight, out, k_held, v_held, terms, sems, out_sems):
    columns = out.shape[2]
    n = out.shape[0]
    spans = [pl.ds(j * columns, columns) for j in range(n)]
    k_in = fetch([(key_weight.at[p], k_held.at[p]) for p in spans], sems.at[0])
    v_in = fetch([(value_weight.at[p], v_held.at[p]) for p in spans], sems.at[1])
    outs = []
    for j in range(n):
        k_in[j].wait()
        v_in[j].wait()
        t = lax.dot_general(grad[:, :DH], k_held[spans[j], :], NT, preferred_element_type=f32)
        t += lax.dot_general(grad[:, DH:], v_held[spans[j], :], NT, preferred_element_type=f32)
        terms[j] = t.astype(bf16)
        copy = pltpu.make_async_copy(terms.at[j], out.at[j], out_sems.at[j])
        copy.start()
        outs.append(copy)
    for copy in outs:
        copy.wait()


def input_terms(grad, key_weight, value_weight, heads):
    rows = grad.shape[0]
    shape = (heads, rows, key_weight.shape[0] // heads)
    return pl.pallas_call(
        input_terms_kernel,
        out_shape=jax.ShapeDtypeStruct(shape, bf16),
        in_specs=[VMEM, ANY, ANY],
        out_specs=ANY,
        scratch_shapes=[
            pltpu.VMEM(key_weight.shape, bf16),
            pltpu.VMEM(key_weight.shape, bf16),
            pltpu.VMEM(shape, bf16),
            pltpu.SemaphoreType.DMA((2, heads)),
            pltpu.SemaphoreType.DMA((heads,)),
        ],
        compiler_params=pltpu.CompilerParams(vmem_limit_bytes=BIG),
        cost_estimate=pl.CostEstimate(
            flops=4 * rows * DH * key_weight.shape[0], bytes_accessed=6 * 2**20, transcendentals=0
        ),
    )(grad, key_weight, value_weight)


def weight_terms_kernel(at, g0, g1, g2, g3, x0, x1, x2, x3, *refs):
    *outs, held, turned, sems = refs
    z = at[0]
    copies = fetch([(x, held.at[i]) for i, x in enumerate((x0, x1, x2, x3))], sems)
    rows = g0.shape[0]
    for i, g in enumerate((g0, g1, g2, g3)):
        turned[:, i * rows:(i + 1) * rows] = g[...].T
    for copy in copies:
        copy.wait()
    n_z = len(outs)
    for k in reversed(range(n_z)):
        to = lax.rem(z + k, n_z)
        terms = jnp.dot(turned[:, :rows], held[0, to], preferred_element_type=f32)
        for i in range(1, 4):
            terms += jnp.dot(
                turned[:, i * rows:(i + 1) * rows], held[i, to], preferred_element_type=f32
            )
        outs[k][...] = terms.astype(outs[k].dtype)


def weight_terms(at, grads, cuts):
    rows, columns = grads[0].shape
    n_z = cuts[0].shape[0]
    shape = (columns, cuts[0].shape[2])
    return pl.pallas_call(
        weight_terms_kernel,
        out_shape=[jax.ShapeDtypeStruct(shape, bf16 if k else f32) for k in range(n_z)],
        in_specs=[SMEM] + [VMEM] * 4 + [ANY] * 4,
        out_specs=[VMEM] * n_z,
        scratch_shapes=[
            pltpu.VMEM((4,) + cuts[0].shape, bf16),
            pltpu.VMEM((columns, 4 * rows), bf16),
            pltpu.SemaphoreType.DMA((4,)),
        ],
        compiler_params=pltpu.CompilerParams(vmem_limit_bytes=MIDDLE),
        cost_estimate=pl.CostEstimate(
            flops=8 * rows * n_z * shape[0] * shape[1], bytes_accessed=4 * 2**20, transcendentals=0
        ),
    )(at, *grads, *cuts)


def weight_sum_kernel(*refs):
    *parts, key_out, value_out = refs
    total = parts[0][...]
    for part in parts[1:]:
        total += part[...].astype(f32)
    key_out[...] = total[:DH, :].T
    value_out[...] = total[DH:, :].T


def weight_sum(parts):
    shape = jax.ShapeDtypeStruct((parts[0].shape[1], DH), f32)
    return pl.pallas_call(
        weight_sum_kernel,
        out_shape=(shape, shape),
        in_specs=[VMEM] * len(parts),
        out_specs=(VMEM, VMEM),
        compiler_params=pltpu.CompilerParams(vmem_limit_bytes=SMALL),
    )(*parts)


def swap(x, axis):
    return lax.ppermute(x, axis, [(0, 1), (1, 0)])


def cross(x):
    return lax.ppermute(x, ("xh", "core"), [(0, 3), (1, 2), (2, 1), (3, 0)])


def on_device(
    queries_one, grads_one, queries_two, grads_two, key_rows, value_rows,
    shared_input, key_weight, value_weight, block_order,
):
    rows, width = shared_input.shape
    n_xh, n_z, n_core, n_xl, n_y = (lax.axis_size(a) for a in CTX + HEAD)
    heads = n_xl * n_y
    core, xh, z = lax.axis_index("core"), lax.axis_index("xh"), lax.axis_index("z")
    head = lax.axis_index(HEAD)

    def slot(h, at, c):
        return 2 * ((h * n_z + at) * n_core + c)

    where = jnp.stack(
        [slot(xh, z, core), slot(1 - xh, z, core), slot(xh, z, 1 - core), slot(1 - xh, z, 1 - core)]
        + [slot(xh, b, core) for b in range(n_z)]
    ).astype(jnp.int32)

    at = jnp.stack([xh, core]).astype(jnp.int32)

    with jax.named_scope("gather"):
        own, packed, *cuts = pack(
            at, (queries_one, grads_one, queries_two, grads_two), key_rows, value_rows, shared_input, n_z
        )
        packed = lax.all_to_all(packed, "z", 0, 0)
        far = swap(own, "xh")
        side = swap(own, "core")
        both = swap(far, "core")
        where, packed = lax.optimization_barrier((where, packed))
    with jax.named_scope("spread_input"):
        far, *cuts = lax.optimization_barrier((far, *cuts))
        cuts = [cuts[0], swap(cuts[1], "xh"), swap(cuts[2], "core"), cross(cuts[3])]

    with jax.named_scope("attention_stats"):
        stats = attention_stats(block_order, where, own, far, side, both, packed)
    with jax.named_scope("share_stats"):
        stats, *cuts = lax.optimization_barrier((stats, *cuts))
        stats = (stats, swap(stats, "xh"), swap(stats, "core"), cross(stats))
    with jax.named_scope("attention_grads"):
        dq_own, dq_far, dq_pair, dkv = attention_grads(
            block_order, where, own, far, side, both, packed, stats
        )
    with jax.named_scope("scatter_grads"):
        dkv = lax.all_to_all(dkv, "z", 0, 0)
    with jax.named_scope("query_grads"):
        dq_pair = swap(dq_pair, "core").astype(f32)
        dq_own = dq_own + dq_pair[0]
        dq_far = swap((dq_far + dq_pair[1]).astype(bf16), "xh")
        dkv, dq_own, dq_far = lax.optimization_barrier((dkv, dq_own, dq_far))
        dq = (dq_own + dq_far.astype(f32)).astype(bf16)
        dq_one, dq_two = dq[:, :GROUP * DH], dq[:, GROUP * DH:]
    with jax.named_scope("scatter_grads"):
        grad = key_sum(dkv)

        grads = [grad, swap(grad, "xh"), swap(grad, "core"), cross(grad)]

    with jax.named_scope("input_grad"):
        terms = input_terms(grad, key_weight, value_weight, heads)
        terms = lax.all_to_all(terms, HEAD, 0, 0)
        input_grad = jnp.sum(terms.astype(f32), axis=0).astype(bf16)

    with jax.named_scope("weight_grad"):
        own, *rest = weight_terms(z.astype(jnp.int32).reshape(1), grads, cuts)
        parts = [own] + [
            lax.ppermute(part, "z", [(i, (i + k) % n_z) for i in range(n_z)])
            for k, part in enumerate(rest, 1)
        ]
        key_weight_grad, value_weight_grad = weight_sum(parts)
    return (dq_one, dq_two, input_grad, key_weight_grad, value_weight_grad)


def solution(mesh):
    fine = Mesh(mesh.devices.reshape(2, 8, 2, 2, 4), CTX + HEAD)
    both = P(CTX, HEAD)
    return jax.shard_map(
        on_device,
        mesh=fine,
        in_specs=(both,) * 6 + (P(CTX, None), P(None, HEAD), P(None, HEAD), P()),
        out_specs=(both,) * 5,
        check_vma=False,
    )
```

profile of v0, /device:TPU:24, one launch (start us, length us, event | category | flops | bytes accessed | tf_op | source)
XLA Modules:
  0.0 172.6 jit_solution(8889566035291621401)
XLA Ops:
  0.6 0.6 pad_add_fusion.at
  1.2 4.8 %gather.1 = (bf16[128,2048]{1,0:T(8,128)(2,1)}, bf16[8,128,256]{2,1,0:T(8,128)(2,1)}, bf16[8,128,256]{2,1,0:T(8,128)(2,1)}, bf16[8,128,256]{2,1,0:T(8,128)(2,1)}...) custom-call(s32[2]{0:T(128)} %pad_add_fusion.at, bf16[128,512]{1,0:T(8,128)(2,1)} %refs_0_.1, ...), custom_call_target="tpu_custom_call" | custom-call | tf_op jit(solution)/shard_map/gather/pallas_call | solution.py:342
  6.1 3.1 %collective-permute-start = (bf16[128,2048]{1,0:T(8,128)(2,1)}, bf16[128,2048]{1,0:T(8,128)(2,1)S(1)}, u32[]{:S(2)}, u32[]{:S(2)}) collective-permute-start(bf16[128,2048]{1,0:T(8,128)(2,1)} %get-tuple-element.42.own), channel_id=1, source_target_pairs={{0,128},{128,0},{1,129},{129,1},{2,130},{130,2},{3,131},{131,3},{4... | collective-permute-start | bytes 1572872 | tf_op jit(solution)/shard_map/gather/ppermute | solution.py:477
  9.2 8.5 %all-to-all-start = ((bf16[8,128,256]{2,1,0:T(8,128)(2,1)}), bf16[8,128,256]{2,1,0:T(8,128)(2,1)S(1)}, u32[]{:S(2)}, u32[]{:S(2)}) async-start(bf16[8,128,256]{2,1,0:T(8,128)(2,1)} %get-tuple-element.40), calls=%async_computation | async-start | bytes 1048576 | tf_op jit(solution)/shard_map/gather/all_to_all | solution.py:508
  17.6 0.0 collective-permute-start.1
  17.7 3.9 %collective-permute-done.far = bf16[128,2048]{1,0:T(8,128)(2,1)S(1)} collective-permute-done((bf16[128,2048]{1,0:T(8,128)(2,1)}, bf16[128,2048]{1,0:T(8,128)(2,1)S(1)}, u32[]{:S(2)}, u32[]{:S(2)}) %collective-permute-start) | collective-permute-done | bytes 524320 | tf_op jit(solution)/shard_map/gather/ppermute | solution.py:477
  21.5 0.0 collective-permute-start.2
  21.5 3.0 %collective-permute-start.3 = (bf16[8,128,256]{2,1,0:T(8,128)(2,1)}, bf16[8,128,256]{2,1,0:T(8,128)(2,1)S(1)}, u32[]{:S(2)}, u32[]{:S(2)}) collective-permute-start(bf16[8,128,256]{2,1,0:T(8,128)(2,1)} %get-tuple-element.50), channel_id=1, source_target_pairs={{0,128},{128,0},{1,129},{129,1},{2,130},{130,2},{3,131},{131,3},{4... | collective-permute-start | bytes 1572872 | tf_op jit(solution)/shard_map/spread_input/ppermute | solution.py:477
  24.6 0.2 collective-permute-start.4
  24.8 0.4 collective-permute-start.5
  25.2 0.6 stack.60.where
  25.8 9.1 %all-to-all-done.packed = bf16[8,128,256]{2,1,0:T(8,128)(2,1)S(1)} async-done(((bf16[8,128,256]{2,1,0:T(8,128)(2,1)}), bf16[8,128,256]{2,1,0:T(8,128)(2,1)S(1)}, u32[]{:S(2)}, u32[]{:S(2)}) %all-to-all-start) | async-done | bytes 524320 | tf_op jit(solution)/shard_map/gather/all_to_all | solution.py:508
  34.9 0.0 collective-permute-done.1.side
  34.9 0.0 collective-permute-done.2.both
  34.9 0.8 copy-done.3
  35.7 0.2 copy-done.6
  35.9 10.3 %attention_stats.1.s_own = f32[3,8,512]{2,1,0:T(8,128)} custom-call(s32[64]{0:T(128)} %order.3, s32[12]{0:T(128)} %stack.60.where, bf16[128,2048]{1,0:T(8,128)(2,1)} %get-tuple-element.42.own, bf16[128,2048]{1,0:T(8,128)(2,1)} %copy-done.5, bf16[128,2048]{1,0:T(8,128)(2,1)} %copy-done.6, bf16[128,2048]{1,0:T(8,128)(2,1)} %collective-permute-done.2.both, ...), custom_call_target="tpu_custom_call" | custom-call | flops 1073741824 | bytes 8388608 | tf_op jit(solution)/shard_map/attention_stats/pallas_call | solution.py:276
  46.2 0.0 collective-permute-done.4.x2
  46.2 2.2 %collective-permute-done.5.x3 = bf16[8,128,256]{2,1,0:T(8,128)(2,1)S(1)} collective-permute-done((bf16[8,128,256]{2,1,0:T(8,128)(2,1)}, bf16[8,128,256]{2,1,0:T(8,128)(2,1)S(1)}, u32[]{:S(2)}, u32[]{:S(2)}) %collective-permute-start.5) | collective-permute-done | bytes 524320 | tf_op jit(solution)/shard_map/spread_input/ppermute | solution.py:481
  48.4 2.8 %collective-permute-start.8 = (f32[3,8,512]{2,1,0:T(8,128)}, f32[3,8,512]{2,1,0:T(8,128)S(1)}, u32[]{:S(2)}, u32[]{:S(2)}) collective-permute-start(f32[3,8,512]{2,1,0:T(8,128)} %attention_stats.1.s_own), channel_id=1, source_target_pairs={{0,136},{8,128},{128,8},{136,0},{1,137},{9,129},{129,9},{137,1},{2... | collective-permute-start | bytes 147464 | tf_op jit(solution)/shard_map/share_stats/ppermute | solution.py:481
  51.3 0.3 collective-permute-start.7
  51.6 0.5 collective-permute-start.6
  52.1 1.8 %collective-permute-done.8.s_both = f32[3,8,512]{2,1,0:T(8,128)S(1)} collective-permute-done((f32[3,8,512]{2,1,0:T(8,128)}, f32[3,8,512]{2,1,0:T(8,128)S(1)}, u32[]{:S(2)}, u32[]{:S(2)}) %collective-permute-start.8) | collective-permute-done | bytes 49184 | tf_op jit(solution)/shard_map/share_stats/ppermute | solution.py:481
  53.9 3.5 %collective-permute-done.6.s_far = f32[3,8,512]{2,1,0:T(8,128)S(1)} collective-permute-done((f32[3,8,512]{2,1,0:T(8,128)}, f32[3,8,512]{2,1,0:T(8,128)S(1)}, u32[]{:S(2)}, u32[]{:S(2)}) %collective-permute-start.6) | collective-permute-done | bytes 49184 | tf_op jit(solution)/shard_map/share_stats/ppermute | solution.py:477
  57.4 0.6 copy-done.9
  58.0 12.8 %attention_grads.1 = (f32[128,1024]{1,0:T(8,128)}, f32[128,1024]{1,0:T(8,128)}, bf16[2,128,1024]{2,1,0:T(8,128)(2,1)}, bf16[8,128,256]{2,1,0:T(8,128)(2,1)}) custom-call(s32[64]{0:T(128)} %order.3, s32[12]{0:T(128)} %stack.60.where, bf16[128,2048]{1,0:T(8,128)(2,1)} %get-tuple-element.42.own, bf16[128,2048]{1,0:T(8,128)(2,1)} %copy-done.5, ...), custom_call_target="tpu_custom_call" | custom-call | flops 2684354560 | bytes 8388608 | tf_op jit(solution)/shard_map/attention_grads/pallas_call | solution.py:293
  70.8 0.3 collective-permute-start.9
  71.1 9.0 %all-to-all-start.1 = ((bf16[8,128,256]{2,1,0:T(8,128)(2,1)}), bf16[8,128,256]{2,1,0:T(8,128)(2,1)S(1)}, u32[]{:S(2)}, u32[]{:S(2)}) async-start(bf16[8,128,256]{2,1,0:T(8,128)(2,1)} %get-tuple-element.54), calls=%async_computation.1 | async-start | bytes 1048576 | tf_op jit(solution)/shard_map/scatter_grads/all_to_all | solution.py:527
  80.1 0.1 convert_element_type.14
  80.2 1.2 fusion.1
  81.4 1.5 collective-permute-start.10
  82.9 8.5 %collective-permute-done.10 = bf16[128,1024]{1,0:T(8,128)(2,1)S(1)} collective-permute-done((bf16[128,1024]{1,0:T(8,128)(2,1)S(1)}, bf16[128,1024]{1,0:T(8,128)(2,1)S(1)}, u32[]{:S(2)}, u32[]{:S(2)}) %collective-permute-start.10) | collective-permute-done | bytes 262176 | tf_op jit(solution)/shard_map/query_grads/ppermute | solution.py:477
  91.4 6.9 %all-to-all-done.1.parts = bf16[8,128,256]{2,1,0:T(8,128)(2,1)S(1)} async-done(((bf16[8,128,256]{2,1,0:T(8,128)(2,1)}), bf16[8,128,256]{2,1,0:T(8,128)(2,1)S(1)}, u32[]{:S(2)}, u32[]{:S(2)}) %all-to-all-start.1) | async-done | bytes 524320 | tf_op jit(solution)/shard_map/scatter_grads/all_to_all | solution.py:527
  98.3 0.1 scatter_grads.1.grad.g0
  98.4 0.0 copy-start
  98.4 0.6 copy-done
  99.0 5.8 %input_grad.1 = bf16[8,128,1024]{2,1,0:T(8,128)(2,1)} custom-call(bf16[128,256]{1,0:T(8,128)(2,1)} %copy-done, bf16[8192,128]{1,0:T(8,128)(2,1)} %key_weight.1, bf16[8192,128]{1,0:T(8,128)(2,1)} %value_weight.1), custom_call_target="tpu_custom_call" | custom-call | flops 536870912 | bytes 6291456 | tf_op jit(solution)/shard_map/input_grad/pallas_call | solution.py:396
  104.8 0.0 copy-start.1
  104.8 4.9 %all-to-all-start.2 = ((bf16[8,128,1024]{2,1,0:T(8,128)(2,1)}), bf16[8,128,1024]{2,1,0:T(8,128)(2,1)}, u32[]{:S(2)}, u32[]{:S(2)}) async-start(bf16[8,128,1024]{2,1,0:T(8,128)(2,1)} %input_grad.1), calls=%async_computation.2 | async-start | bytes 4194304 | tf_op jit(solution)/shard_map/input_grad/all_to_all | solution.py:542
  109.7 1.6 collective-permute-start.13
  111.3 1.0 collective-permute-start.12
  112.3 1.0 collective-permute-start.11
  113.3 22.5 %collective-permute-done.13.g3 = bf16[128,256]{1,0:T(8,128)(2,1)S(1)} collective-permute-done((bf16[128,256]{1,0:T(8,128)(2,1)S(1)}, bf16[128,256]{1,0:T(8,128)(2,1)S(1)}, u32[]{:S(2)}, u32[]{:S(2)}) %collective-permute-start.13) | collective-permute-done | bytes 65568 | tf_op jit(solution)/shard_map/scatter_grads/ppermute | solution.py:481
  135.8 0.0 collective-permute-done.12.g2
  135.8 2.6 %collective-permute-done.11.g1 = bf16[128,256]{1,0:T(8,128)(2,1)S(1)} collective-permute-done((bf16[128,256]{1,0:T(8,128)(2,1)S(1)}, bf16[128,256]{1,0:T(8,128)(2,1)S(1)}, u32[]{:S(2)}, u32[]{:S(2)}) %collective-permute-start.11) | collective-permute-done | bytes 65568 | tf_op jit(solution)/shard_map/scatter_grads/ppermute | solution.py:477
  138.4 1.5 weight_grad.2
  140.0 0.1 collective-permute-start.14
  140.1 0.1 collective-permute-start.15
  140.2 0.1 add_convert_fusion
  140.2 3.1 %collective-permute-start.16 = (bf16[256,256]{1,0:T(8,128)(2,1)S(1)}, bf16[256,256]{1,0:T(8,128)(2,1)S(1)}, u32[]{:S(2)}, u32[]{:S(2)}) collective-permute-start(bf16[256,256]{1,0:T(8,128)(2,1)S(1)} %get-tuple-element.68), channel_id=1, source_target_pairs={{0,48},{16,64},{32,80},{48,96},{64,112},{80,0},{96,16},{112,32},{1... | collective-permute-start | bytes 393224 | tf_op jit(solution)/shard_map/weight_grad/ppermute | solution.py:548
  143.4 3.3 %collective-permute-start.17 = (bf16[256,256]{1,0:T(8,128)(2,1)S(1)}, bf16[256,256]{1,0:T(8,128)(2,1)S(1)}, u32[]{:S(2)}, u32[]{:S(2)}) collective-permute-start(bf16[256,256]{1,0:T(8,128)(2,1)S(1)} %get-tuple-element.69), channel_id=1, source_target_pairs={{0,64},{16,80},{32,96},{48,112},{64,0},{80,16},{96,32},{112,48},{1... | collective-permute-start | bytes 393224 | tf_op jit(solution)/shard_map/weight_grad/ppermute | solution.py:548
  146.7 1.2 collective-permute-start.18
  147.9 2.4 %collective-permute-done.14.refs_1_ = bf16[256,256]{1,0:T(8,128)(2,1)S(1)} collective-permute-done((bf16[256,256]{1,0:T(8,128)(2,1)S(1)}, bf16[256,256]{1,0:T(8,128)(2,1)S(1)}, u32[]{:S(2)}, u32[]{:S(2)}) %collective-permute-start.14) | collective-permute-done | bytes 131104 | tf_op jit(solution)/shard_map/weight_grad/ppermute | solution.py:548
  150.3 0.6 collective-permute-start.19
  150.8 2.1 %collective-permute-done.15.refs_2_ = bf16[256,256]{1,0:T(8,128)(2,1)S(1)} collective-permute-done((bf16[256,256]{1,0:T(8,128)(2,1)S(1)}, bf16[256,256]{1,0:T(8,128)(2,1)S(1)}, u32[]{:S(2)}, u32[]{:S(2)}) %collective-permute-start.15) | collective-permute-done | bytes 131104 | tf_op jit(solution)/shard_map/weight_grad/ppermute | solution.py:548
  153.0 4.2 %collective-permute-start.20 = (bf16[256,256]{1,0:T(8,128)(2,1)S(1)}, bf16[256,256]{1,0:T(8,128)(2,1)S(1)}, u32[]{:S(2)}, u32[]{:S(2)}) collective-permute-start(bf16[256,256]{1,0:T(8,128)(2,1)S(1)} %get-tuple-element.72), channel_id=1, source_target_pairs={{0,112},{16,0},{32,16},{48,32},{64,48},{80,64},{96,80},{112,96},{1... | collective-permute-start | bytes 393224 | tf_op jit(solution)/shard_map/weight_grad/ppermute | solution.py:548
  157.2 0.7 fusion.3
  157.9 5.0 %collective-permute-done.16.refs_3_ = bf16[256,256]{1,0:T(8,128)(2,1)S(1)} collective-permute-done((bf16[256,256]{1,0:T(8,128)(2,1)S(1)}, bf16[256,256]{1,0:T(8,128)(2,1)S(1)}, u32[]{:S(2)}, u32[]{:S(2)}) %collective-permute-start.16) | collective-permute-done | bytes 131104 | tf_op jit(solution)/shard_map/weight_grad/ppermute | solution.py:548
  162.9 0.0 collective-permute-done.18.refs_5_
  162.9 3.9 %collective-permute-done.19.refs_6_ = bf16[256,256]{1,0:T(8,128)(2,1)S(1)} collective-permute-done((bf16[256,256]{1,0:T(8,128)(2,1)S(1)}, bf16[256,256]{1,0:T(8,128)(2,1)S(1)}, u32[]{:S(2)}, u32[]{:S(2)}) %collective-permute-start.19) | collective-permute-done | bytes 131104 | tf_op jit(solution)/shard_map/weight_grad/ppermute | solution.py:548
  166.8 2.2 %collective-permute-done.20.refs_7_ = bf16[256,256]{1,0:T(8,128)(2,1)S(1)} collective-permute-done((bf16[256,256]{1,0:T(8,128)(2,1)S(1)}, bf16[256,256]{1,0:T(8,128)(2,1)S(1)}, u32[]{:S(2)}, u32[]{:S(2)}) %collective-permute-start.20) | collective-permute-done | bytes 131104 | tf_op jit(solution)/shard_map/weight_grad/ppermute | solution.py:548
  169.0 0.8 weight_grad.3
  169.9 0.0 all-to-all-done.2
  169.9 2.7 %reduce_sum.12 = bf16[128,1024]{1,0:T(8,128)(2,1)} reduce(bf16[8,128,1024]{2,1,0:T(8,128)(2,1)} %all-to-all-done.2, bf16[]{:T(256)} %constant.34.clone.1), dimensions={0}, to_apply=%region_0.0 | reduce | flops 917504 | bytes 2359298 | tf_op jit(solution)/shard_map/input_grad/reduce_sum | solution.py:543
  (18 shorter events, 0.0 us)
Async XLA Ops:
  6.1 15.5 %collective-permute-start = (bf16[128,2048]{1,0:T(8,128)(2,1)}, bf16[128,2048]{1,0:T(8,128)(2,1)S(1)}, u32[]{:S(2)}, u32[]{:S(2)}) collective-permute-start(bf16[128,2048]{1,0:T(8,128)(2,1)} %get-tuple-element.42.own), channel_id=1, source_target_pairs={{0,128},{128,0},{1,129},{129,1},{2,130},{130,2},{3,131},{131,3},{4... | collective-permute-start | bytes 1572872 | tf_op jit(solution)/shard_map/gather/ppermute | solution.py:477
  9.2 25.7 %all-to-all-start = ((bf16[8,128,256]{2,1,0:T(8,128)(2,1)}), bf16[8,128,256]{2,1,0:T(8,128)(2,1)S(1)}, u32[]{:S(2)}, u32[]{:S(2)}) async-start(bf16[8,128,256]{2,1,0:T(8,128)(2,1)} %get-tuple-element.40), calls=%async_computation | async-start | bytes 1048576 | tf_op jit(solution)/shard_map/gather/all_to_all | solution.py:508
  17.6 17.2 %collective-permute-start.1 = (bf16[128,2048]{1,0:T(8,128)(2,1)}, bf16[128,2048]{1,0:T(8,128)(2,1)S(1)}, u32[]{:S(2)}, u32[]{:S(2)}) collective-permute-start(bf16[128,2048]{1,0:T(8,128)(2,1)} %get-tuple-element.42.own), channel_id=1, source_target_pairs={{0,8},{8,0},{1,9},{9,1},{2,10},{10,2},{3,11},{11,3},{4,12},{12,4},... | collective-permute-start | bytes 1572872 | tf_op jit(solution)/shard_map/gather/ppermute | solution.py:477
  21.5 13.3 %copy-start.5 = (bf16[128,2048]{1,0:T(8,128)(2,1)}, bf16[128,2048]{1,0:T(8,128)(2,1)S(1)}, u32[]{:S(2)}) copy-start(bf16[128,2048]{1,0:T(8,128)(2,1)S(1)} %collective-permute-done.far) | copy-start | bytes 1572868
  21.5 13.3 %collective-permute-start.2 = (bf16[128,2048]{1,0:T(8,128)(2,1)S(1)}, bf16[128,2048]{1,0:T(8,128)(2,1)}, u32[]{:S(2)}, u32[]{:S(2)}) collective-permute-start(bf16[128,2048]{1,0:T(8,128)(2,1)S(1)} %collective-permute-done.far), channel_id=1, source_target_pairs={{0,8},{8,0},{1,9},{9,1},{2,10},{10,2},{3,11},{11,3},{4,12},{12,4},... | collective-permute-start | bytes 1572872 | tf_op jit(solution)/shard_map/gather/ppermute | solution.py:477
  21.5 24.7 %collective-permute-start.3 = (bf16[8,128,256]{2,1,0:T(8,128)(2,1)}, bf16[8,128,256]{2,1,0:T(8,128)(2,1)S(1)}, u32[]{:S(2)}, u32[]{:S(2)}) collective-permute-start(bf16[8,128,256]{2,1,0:T(8,128)(2,1)} %get-tuple-element.50), channel_id=1, source_target_pairs={{0,128},{128,0},{1,129},{129,1},{2,130},{130,2},{3,131},{131,3},{4... | collective-permute-start | bytes 1572872 | tf_op jit(solution)/shard_map/spread_input/ppermute | solution.py:477
  24.6 21.6 %collective-permute-start.4 = (bf16[8,128,256]{2,1,0:T(8,128)(2,1)}, bf16[8,128,256]{2,1,0:T(8,128)(2,1)S(1)}, u32[]{:S(2)}, u32[]{:S(2)}) collective-permute-start(bf16[8,128,256]{2,1,0:T(8,128)(2,1)} %get-tuple-element.51), channel_id=1, source_target_pairs={{0,8},{8,0},{1,9},{9,1},{2,10},{10,2},{3,11},{11,3},{4,12},{12,4},... | collective-permute-start | bytes 1572872 | tf_op jit(solution)/shard_map/spread_input/ppermute | solution.py:477
  24.8 23.6 %collective-permute-start.5 = (bf16[8,128,256]{2,1,0:T(8,128)(2,1)}, bf16[8,128,256]{2,1,0:T(8,128)(2,1)S(1)}, u32[]{:S(2)}, u32[]{:S(2)}) collective-permute-start(bf16[8,128,256]{2,1,0:T(8,128)(2,1)} %get-tuple-element.52), channel_id=1, source_target_pairs={{0,136},{8,128},{128,8},{136,0},{1,137},{9,129},{129,9},{137,1},{2... | collective-permute-start | bytes 1572872 | tf_op jit(solution)/shard_map/spread_input/ppermute | solution.py:481
  34.9 0.8 copy-start.3
  34.9 1.0 copy-start.6
  48.4 5.5 %collective-permute-start.8 = (f32[3,8,512]{2,1,0:T(8,128)}, f32[3,8,512]{2,1,0:T(8,128)S(1)}, u32[]{:S(2)}, u32[]{:S(2)}) collective-permute-start(f32[3,8,512]{2,1,0:T(8,128)} %attention_stats.1.s_own), channel_id=1, source_target_pairs={{0,136},{8,128},{128,8},{136,0},{1,137},{9,129},{129,9},{137,1},{2... | collective-permute-start | bytes 147464 | tf_op jit(solution)/shard_map/share_stats/ppermute | solution.py:481
  51.3 2.6 %collective-permute-start.7 = (f32[3,8,512]{2,1,0:T(8,128)}, f32[3,8,512]{2,1,0:T(8,128)S(1)}, u32[]{:S(2)}, u32[]{:S(2)}) collective-permute-start(f32[3,8,512]{2,1,0:T(8,128)} %attention_stats.1.s_own), channel_id=1, source_target_pairs={{0,8},{8,0},{1,9},{9,1},{2,10},{10,2},{3,11},{11,3},{4,12},{12,4},... | collective-permute-start | bytes 147464 | tf_op jit(solution)/shard_map/share_stats/ppermute | solution.py:477
  51.6 5.8 %collective-permute-start.6 = (f32[3,8,512]{2,1,0:T(8,128)}, f32[3,8,512]{2,1,0:T(8,128)S(1)}, u32[]{:S(2)}, u32[]{:S(2)}) collective-permute-start(f32[3,8,512]{2,1,0:T(8,128)} %attention_stats.1.s_own), channel_id=1, source_target_pairs={{0,128},{128,0},{1,129},{129,1},{2,130},{130,2},{3,131},{131,3},{4... | collective-permute-start | bytes 147464 | tf_op jit(solution)/shard_map/share_stats/ppermute | solution.py:477
  53.9 3.5 %copy-start.7 = (f32[3,8,512]{2,1,0:T(8,128)}, f32[3,8,512]{2,1,0:T(8,128)S(1)}, u32[]{:S(2)}) copy-start(f32[3,8,512]{2,1,0:T(8,128)S(1)} %collective-permute-done.8.s_both) | copy-start | bytes 147460
  53.9 3.5 %copy-start.8 = (f32[3,8,512]{2,1,0:T(8,128)}, f32[3,8,512]{2,1,0:T(8,128)S(1)}, u32[]{:S(2)}) copy-start(f32[3,8,512]{2,1,0:T(8,128)S(1)} %collective-permute-done.7.s_side) | copy-start | bytes 147460
  57.4 0.6 copy-start.9
  70.8 9.4 %copy-start.4 = (f32[128,1024]{1,0:T(8,128)S(1)}, f32[128,1024]{1,0:T(8,128)}, u32[]{:S(2)}) copy-start(f32[128,1024]{1,0:T(8,128)} %get-tuple-element.55) | copy-start | bytes 1572868
  70.8 9.3 %collective-permute-start.9 = (bf16[2,128,1024]{2,1,0:T(8,128)(2,1)}, bf16[2,128,1024]{2,1,0:T(8,128)(2,1)S(1)}, u32[]{:S(2)}, u32[]{:S(2)}) collective-permute-start(bf16[2,128,1024]{2,1,0:T(8,128)(2,1)} %get-tuple-element.56), channel_id=1, source_target_pairs={{0,8},{8,0},{1,9},{9,1},{2,10},{10,2},{3,11},{11,3},{4,12},{12,4},... | collective-permute-start | bytes 1572872 | tf_op jit(solution)/shard_map/query_grads/ppermute | solution.py:477
  71.1 27.2 %all-to-all-start.1 = ((bf16[8,128,256]{2,1,0:T(8,128)(2,1)}), bf16[8,128,256]{2,1,0:T(8,128)(2,1)S(1)}, u32[]{:S(2)}, u32[]{:S(2)}) async-start(bf16[8,128,256]{2,1,0:T(8,128)(2,1)} %get-tuple-element.54), calls=%async_computation.1 | async-start | bytes 1048576 | tf_op jit(solution)/shard_map/scatter_grads/all_to_all | solution.py:527
  81.4 10.0 %collective-permute-start.10 = (bf16[128,1024]{1,0:T(8,128)(2,1)S(1)}, bf16[128,1024]{1,0:T(8,128)(2,1)S(1)}, u32[]{:S(2)}, u32[]{:S(2)}) collective-permute-start(bf16[128,1024]{1,0:T(8,128)(2,1)S(1)} %get-tuple-element.75), channel_id=1, source_target_pairs={{0,128},{128,0},{1,129},{129,1},{2,130},{130,2},{3,131},{131,3},{4... | collective-permute-start | bytes 786440 | tf_op jit(solution)/shard_map/query_grads/ppermute | solution.py:477
  98.4 0.6 copy-start
  104.8 4.9 %copy-start.1 = (bf16[128,256]{1,0:T(8,128)(2,1)S(1)}, bf16[128,256]{1,0:T(8,128)(2,1)}, u32[]{:S(2)}) copy-start(bf16[128,256]{1,0:T(8,128)(2,1)} %copy-done) | copy-start | bytes 196612
  104.8 33.6 %copy-start.2 = (bf16[8,128,256]{2,1,0:T(8,128)(2,1)S(1)}, bf16[8,128,256]{2,1,0:T(8,128)(2,1)}, u32[]{:S(2)}) copy-start(bf16[8,128,256]{2,1,0:T(8,128)(2,1)} %get-tuple-element.61.x0) | copy-start | bytes 1572868
  104.8 65.1 %all-to-all-start.2 = ((bf16[8,128,1024]{2,1,0:T(8,128)(2,1)}), bf16[8,128,1024]{2,1,0:T(8,128)(2,1)}, u32[]{:S(2)}, u32[]{:S(2)}) async-start(bf16[8,128,1024]{2,1,0:T(8,128)(2,1)} %input_grad.1), calls=%async_computation.2 | async-start | bytes 4194304 | tf_op jit(solution)/shard_map/input_grad/all_to_all | solution.py:542
  109.7 26.1 %collective-permute-start.13 = (bf16[128,256]{1,0:T(8,128)(2,1)S(1)}, bf16[128,256]{1,0:T(8,128)(2,1)S(1)}, u32[]{:S(2)}, u32[]{:S(2)}) collective-permute-start(bf16[128,256]{1,0:T(8,128)(2,1)S(1)} %copy-done.1), channel_id=1, source_target_pairs={{0,136},{8,128},{128,8},{136,0},{1,137},{9,129},{129,9},{137,1},{2... | collective-permute-start | bytes 196616 | tf_op jit(solution)/shard_map/scatter_grads/ppermute | solution.py:481
  111.3 24.5 %collective-permute-start.12 = (bf16[128,256]{1,0:T(8,128)(2,1)S(1)}, bf16[128,256]{1,0:T(8,128)(2,1)S(1)}, u32[]{:S(2)}, u32[]{:S(2)}) collective-permute-start(bf16[128,256]{1,0:T(8,128)(2,1)S(1)} %copy-done.1), channel_id=1, source_target_pairs={{0,8},{8,0},{1,9},{9,1},{2,10},{10,2},{3,11},{11,3},{4,12},{12,4},... | collective-permute-start | bytes 196616 | tf_op jit(solution)/shard_map/scatter_grads/ppermute | solution.py:477
  112.3 26.1 %collective-permute-start.11 = (bf16[128,256]{1,0:T(8,128)(2,1)S(1)}, bf16[128,256]{1,0:T(8,128)(2,1)S(1)}, u32[]{:S(2)}, u32[]{:S(2)}) collective-permute-start(bf16[128,256]{1,0:T(8,128)(2,1)S(1)} %copy-done.1), channel_id=1, source_target_pairs={{0,128},{128,0},{1,129},{129,1},{2,130},{130,2},{3,131},{131,3},{4... | collective-permute-start | bytes 196616 | tf_op jit(solution)/shard_map/scatter_grads/ppermute | solution.py:477
  140.0 10.3 %collective-permute-start.14 = (bf16[256,256]{1,0:T(8,128)(2,1)S(1)}, bf16[256,256]{1,0:T(8,128)(2,1)S(1)}, u32[]{:S(2)}, u32[]{:S(2)}) collective-permute-start(bf16[256,256]{1,0:T(8,128)(2,1)S(1)} %get-tuple-element.66), channel_id=1, source_target_pairs={{0,16},{16,32},{32,48},{48,64},{64,80},{80,96},{96,112},{112,0},{1... | collective-permute-start | bytes 393224 | tf_op jit(solution)/shard_map/weight_grad/ppermute | solution.py:548
  140.1 12.9 %collective-permute-start.15 = (bf16[256,256]{1,0:T(8,128)(2,1)S(1)}, bf16[256,256]{1,0:T(8,128)(2,1)S(1)}, u32[]{:S(2)}, u32[]{:S(2)}) collective-permute-start(bf16[256,256]{1,0:T(8,128)(2,1)S(1)} %get-tuple-element.67), channel_id=1, source_target_pairs={{0,32},{16,48},{32,64},{48,80},{64,96},{80,112},{96,0},{112,16},{1... | collective-permute-start | bytes 393224 | tf_op jit(solution)/shard_map/weight_grad/ppermute | solution.py:548
  140.2 22.6 %collective-permute-start.16 = (bf16[256,256]{1,0:T(8,128)(2,1)S(1)}, bf16[256,256]{1,0:T(8,128)(2,1)S(1)}, u32[]{:S(2)}, u32[]{:S(2)}) collective-permute-start(bf16[256,256]{1,0:T(8,128)(2,1)S(1)} %get-tuple-element.68), channel_id=1, source_target_pairs={{0,48},{16,64},{32,80},{48,96},{64,112},{80,0},{96,16},{112,32},{1... | collective-permute-start | bytes 393224 | tf_op jit(solution)/shard_map/weight_grad/ppermute | solution.py:548
  143.4 19.5 %collective-permute-start.17 = (bf16[256,256]{1,0:T(8,128)(2,1)S(1)}, bf16[256,256]{1,0:T(8,128)(2,1)S(1)}, u32[]{:S(2)}, u32[]{:S(2)}) collective-permute-start(bf16[256,256]{1,0:T(8,128)(2,1)S(1)} %get-tuple-element.69), channel_id=1, source_target_pairs={{0,64},{16,80},{32,96},{48,112},{64,0},{80,16},{96,32},{112,48},{1... | collective-permute-start | bytes 393224 | tf_op jit(solution)/shard_map/weight_grad/ppermute | solution.py:548
  146.7 16.2 %collective-permute-start.18 = (bf16[256,256]{1,0:T(8,128)(2,1)S(1)}, bf16[256,256]{1,0:T(8,128)(2,1)S(1)}, u32[]{:S(2)}, u32[]{:S(2)}) collective-permute-start(bf16[256,256]{1,0:T(8,128)(2,1)S(1)} %get-tuple-element.70), channel_id=1, source_target_pairs={{0,80},{16,96},{32,112},{48,0},{64,16},{80,32},{96,48},{112,64},{1... | collective-permute-start | bytes 393224 | tf_op jit(solution)/shard_map/weight_grad/ppermute | solution.py:548
  150.3 16.5 %collective-permute-start.19 = (bf16[256,256]{1,0:T(8,128)(2,1)S(1)}, bf16[256,256]{1,0:T(8,128)(2,1)S(1)}, u32[]{:S(2)}, u32[]{:S(2)}) collective-permute-start(bf16[256,256]{1,0:T(8,128)(2,1)S(1)} %get-tuple-element.71), channel_id=1, source_target_pairs={{0,96},{16,112},{32,0},{48,16},{64,32},{80,48},{96,64},{112,80},{1... | collective-permute-start | bytes 393224 | tf_op jit(solution)/shard_map/weight_grad/ppermute | solution.py:548
  153.0 16.1 %collective-permute-start.20 = (bf16[256,256]{1,0:T(8,128)(2,1)S(1)}, bf16[256,256]{1,0:T(8,128)(2,1)S(1)}, u32[]{:S(2)}, u32[]{:S(2)}) collective-permute-start(bf16[256,256]{1,0:T(8,128)(2,1)S(1)} %get-tuple-element.72), channel_id=1, source_target_pairs={{0,112},{16,0},{32,16},{48,32},{64,48},{80,64},{96,80},{112,96},{1... | collective-permute-start | bytes 393224 | tf_op jit(solution)/shard_map/weight_grad/ppermute | solution.py:548
where the time goes:
time: 173 us
  waiting for transfers between devices  76.6 us (44%)
  starting transfers between devices  50.8 us (29%)
  Pallas kernels  36.2 us (21%)
  other arithmetic  4.65 us (3%)
  local copies, waits for them, and re-layouts  3.57 us (2%)
    ppermute x3, waiting for transfers between devices, cross(): return lax.ppermute(x, ('xh', 'core'), [(0, 3), (1, 2), (2, 1), (3, 0)])  26.5 us
    ppermute x11, waiting for transfers between devices, swap(): return lax.ppermute(x, axis, [(0, 1), (1, 0)])  18.5 us
    ppermute x7, waiting for transfers between devices, on_device(): lax.ppermute(part, 'z', [(i, (i + k) % n_z) for i in range(n_z)])  15.6 us
    pallas_call x1, Pallas kernels, attention_grads(): pl.pallas_call(grads_kernel, out_shape=(jax.ShapeDtypeStruct(shape, f32),...  12.8 us
    ppermute x7, starting transfers between devices, on_device(): lax.ppermute(part, 'z', [(i, (i + k) % n_z) for i in range(n_z)])  12.7 us
    ppermute x11, starting transfers between devices, swap(): return lax.ppermute(x, axis, [(0, 1), (1, 0)])  11 us
    pallas_call x1, Pallas kernels, attention_stats(): pl.pallas_call(stats_kernel, out_shape=jax.ShapeDtypeStruct((3, 8, width)...  10.3 us
    all_to_all x1, waiting for transfers between devices, on_device(): packed = lax.all_to_all(packed, 'z', 0, 0)  9.06 us
  transfers between devices with their start and end apart: 24, of which 14 were waited for; matrix products, arithmetic and copies ran while one was open for 2% of the time, Pallas kernels for 7%

commit v1 on v0

--- a/solution.py
+++ b/solution.py
@@ -315,18 +315,39 @@
     )(order, where, own, far, side, both, packed, *stats)
 
 
-def pack_kernel(at, *refs):
-    *heads, key_rows, value_rows, x, own, packed = refs[:-5]
-    *cuts, sems = refs[-5:]
+def pack_kernel(*refs):
+    *heads, key_rows, value_rows, own, packed, sems = refs
+    pairs = []
+    for j in range(packed.shape[0]):
+        for i, ref in enumerate((key_rows, value_rows)):
+            pairs.append((ref, packed.at[j, :, i * DH:(i + 1) * DH]))
+    wide = heads[0].shape[1]
+    for i, ref in enumerate(heads):
+        pairs.append((ref, own.at[:, i * wide:(i + 1) * wide]))
+    for copy in fetch(pairs, sems):
+        copy.wait()
+
+
+def pack(heads, key_rows, value_rows, count):
+    rows = key_rows.shape[0]
+    return pl.pallas_call(
+        pack_kernel,
+        in_specs=[ANY] * (len(heads) + 2),
+        out_specs=(VMEM,) * 2,
+        out_shape=(
+            jax.ShapeDtypeStruct((rows, len(heads) * heads[0].shape[1]), bf16),
+            jax.ShapeDtypeStruct((count, rows, 2 * DH), bf16),
+        ),
+        scratch_shapes=[pltpu.SemaphoreType.DMA((2 * count + len(heads),))],
+        compiler_params=pltpu.CompilerParams(vmem_limit_bytes=BIG),
+    )(*heads, key_rows, value_rows)
+
+
+def cut_kernel(at, x, *refs):
+    *cuts, sems = refs
     count, _, wide = cuts[0].shape
     xh, core = at[0], at[1]
     pairs = []
-    for j in range(count):
-        for i, ref in enumerate((key_rows, value_rows)):
-            pairs.append((ref, packed.at[j, :, i * DH:(i + 1) * DH]))
-    side = heads[0].shape[1]
-    for i, ref in enumerate(heads):
-        pairs.append((ref, own.at[:, i * side:(i + 1) * side]))
     for i, cut in enumerate(cuts):
         lead = (xh ^ (i & 1)) * (2 * count) + (core ^ (i >> 1))
         for j in range(count):
@@ -336,21 +357,16 @@
         copy.wait()
 
 
-def pack(at, heads, key_rows, value_rows, x, count):
-    rows = x.shape[0]
-    cut = jax.ShapeDtypeStruct((count, rows, x.shape[1] // (4 * count)), bf16)
-    return pl.pallas_call(
-        pack_kernel,
-        in_specs=[SMEM] + [ANY] * (len(heads) + 3),
-        out_specs=(VMEM,) * 6,
-        out_shape=(
-            jax.ShapeDtypeStruct((rows, len(heads) * heads[0].shape[1]), bf16),
-            jax.ShapeDtypeStruct((count, rows, 2 * DH), bf16),
-            cut, cut, cut, cut,
-        ),
-        scratch_shapes=[pltpu.SemaphoreType.DMA((6 * count + len(heads),))],
+def cut_input(at, x, count):
+    cut = jax.ShapeDtypeStruct((count, x.shape[0], x.shape[1] // (4 * count)), bf16)
+    return pl.pallas_call(
+        cut_kernel,
+        in_specs=[SMEM, ANY],
+        out_specs=(VMEM,) * 4,
+        out_shape=(cut,) * 4,
+        scratch_shapes=[pltpu.SemaphoreType.DMA((4 * count,))],
         compiler_params=pltpu.CompilerParams(vmem_limit_bytes=BIG),
-    )(at, *heads, key_rows, value_rows, x)
+    )(at, x)
 
 
 def key_sum_kernel(parts, grad):
@@ -502,15 +518,17 @@
     at = jnp.stack([xh, core]).astype(jnp.int32)
 
     with jax.named_scope("gather"):
-        own, packed, *cuts = pack(
-            at, (queries_one, grads_one, queries_two, grads_two), key_rows, value_rows, shared_input, n_z
+        own, packed = pack(
+            (queries_one, grads_one, queries_two, grads_two), key_rows, value_rows, n_z
         )
+        shared_input, own = lax.optimization_barrier((shared_input, own))
         packed = lax.all_to_all(packed, "z", 0, 0)
         far = swap(own, "xh")
         side = swap(own, "core")
         both = swap(far, "core")
         where, packed = lax.optimization_barrier((where, packed))
     with jax.named_scope("spread_input"):
+        cuts = cut_input(at, shared_input, n_z)
         far, *cuts = lax.optimization_barrier((far, *cuts))
         cuts = [cuts[0], swap(cuts[1], "xh"), swap(cuts[2], "core"), cross(cuts[3])]
 
@@ -537,8 +555,11 @@
 
         grads = [grad, swap(grad, "xh"), swap(grad, "core"), cross(grad)]
 
+        grads = [grad, swap(grad, "xh"), swap(grad, "core"), cross(grad)]
+
     with jax.named_scope("input_grad"):
         terms = input_terms(grad, key_weight, value_weight, heads)
+        terms, *grads = lax.optimization_barrier((terms, *grads))
         terms = lax.all_to_all(terms, HEAD, 0, 0)
         input_grad = jnp.sum(terms.astype(f32), axis=0).astype(bf16)
 

time: 173 us -> 150 us (0.87)
  waiting for transfers between devices: 76.6 us -> 53.6 us
  starting transfers between devices: 50.8 us -> 47.5 us
  Pallas kernels: 36.2 us -> 38.9 us
    ppermute x3, waiting for transfers between devices: 26.5 us -> 7.96 us  [cross(): return lax.ppermute(x, ('xh', 'core'), [(0, 3), (1, 2), (2, 1), (3, 0)])]
    all_to_all x1, waiting for transfers between devices: 9.06 us -> 4.41 us  [on_device(): packed = lax.all_to_all(packed, 'z', 0, 0)]
    ppermute x7, waiting for transfers between devices: 15.6 us -> 18.2 us  [on_device(): lax.ppermute(part, 'z', [(i, (i + k) % n_z) for i in range(n_z)])]
    ppermute x11, waiting for transfers between devices: 18.5 us -> 16.2 us  [swap(): return lax.ppermute(x, axis, [(0, 1), (1, 0)])]
    ppermute x7, starting transfers between devices: 12.7 us -> 10.4 us  [on_device(): lax.ppermute(part, 'z', [(i, (i + k) % n_z) for i in range(n_z)])]
    pallas_call x1 -> x2, Pallas kernels: 4.84 us -> 6.57 us  [the longest x1 3.88 us: cut_input(): pl.pallas_call(cut_kernel, in_specs=[SMEM, ANY], out_specs=(VMEM,) * 4, o...]
  transfers between devices with their start and end apart: 24 -> 24, of which waited for: 14 -> 13; matrix products, arithmetic and copies ran while one was open for 2% -> 2% of each run, Pallas kernels for 7% -> 15%
where the time goes in v1:
time: 150 us; the launch traced here: 149 us
  waiting for transfers between devices  53.6 us (36%)
  starting transfers between devices  47.5 us (32%)
  Pallas kernels  38.9 us (26%)
  other arithmetic  4.73 us (3%)
  local copies, waits for them, and re-layouts  2.97 us (2%)
    ppermute x7, waiting for transfers between devices, on_device(): lax.ppermute(part, 'z', [(i, (i + k) % n_z) for i in range(n_z)])  18.2 us
    ppermute x11, waiting for transfers between devices, swap(): return lax.ppermute(x, axis, [(0, 1), (1, 0)])  16.2 us
    pallas_call x1, Pallas kernels, attention_grads(): pl.pallas_call(grads_kernel, out_shape=(jax.ShapeDtypeStruct(shape, f32),...  13.3 us
    ppermute x11, starting transfers between devices, swap(): return lax.ppermute(x, axis, [(0, 1), (1, 0)])  11.7 us
    pallas_call x1, Pallas kernels, attention_stats(): pl.pallas_call(stats_kernel, out_shape=jax.ShapeDtypeStruct((3, 8, width)...  10.8 us
    ppermute x7, starting transfers between devices, on_device(): lax.ppermute(part, 'z', [(i, (i + k) % n_z) for i in range(n_z)])  10.4 us
    all_to_all x1, starting transfers between devices, on_device(): packed = lax.all_to_all(packed, 'z', 0, 0)  8.47 us
    all_to_all x1, starting transfers between devices, on_device(): dkv = lax.all_to_all(dkv, 'z', 0, 0)  8.12 us
  transfers between devices with their start and end apart: 24, of which 13 were waited for; matrix products, arithmetic and copies ran while one was open for 2% of the time, Pallas kernels for 15%

profile of v1, /device:TPU:24, one launch (start us, length us, event | category | flops | bytes accessed | tf_op | source)
XLA Modules:
  0.0 148.5 jit_solution(6539158900361945099)
XLA Ops:
  0.6 2.7 %gather.1 = (bf16[128,2048]{1,0:T(8,128)(2,1)}, bf16[8,128,256]{2,1,0:T(8,128)(2,1)}) custom-call(bf16[128,512]{1,0:T(8,128)(2,1)} %refs_0_.1, bf16[128,512]{1,0:T(8,128)(2,1)} %refs_1_.1, bf16[128,512]{1,0:T(8,128)(2,1)} %refs_2_.1, bf16[128,512]{1,0:T(8,128)(2,1)} %refs_3_.1, bf16[128,128]{1,0:T(8,128)(2,1)} %refs_4_.1, bf16[128,128]{1,0:T(8,128)(2,1)} %refs_5_.1), custom_call_target="tpu_custom_call" | custom-call | tf_op jit(solution)/shard_map/gather/pallas_call | solution.py:333
  3.3 3.1 %collective-permute-start = (bf16[128,2048]{1,0:T(8,128)(2,1)}, bf16[128,2048]{1,0:T(8,128)(2,1)S(1)}, u32[]{:S(2)}, u32[]{:S(2)}) collective-permute-start(bf16[128,2048]{1,0:T(8,128)(2,1)} %get-tuple-element.50.own), channel_id=1, source_target_pairs={{0,128},{128,0},{1,129},{129,1},{2,130},{130,2},{3,131},{131,3},{4... | collective-permute-start | bytes 1572872 | tf_op jit(solution)/shard_map/gather/ppermute | solution.py:493
  6.4 8.5 %all-to-all-start = ((bf16[8,128,256]{2,1,0:T(8,128)(2,1)}), bf16[8,128,256]{2,1,0:T(8,128)(2,1)S(1)}, u32[]{:S(2)}, u32[]{:S(2)}) async-start(bf16[8,128,256]{2,1,0:T(8,128)(2,1)} %get-tuple-element.47), calls=%async_computation | async-start | bytes 1048576 | tf_op jit(solution)/shard_map/gather/all_to_all | solution.py:525
  14.9 0.0 collective-permute-start.1
  14.9 3.9 %collective-permute-done.far = bf16[128,2048]{1,0:T(8,128)(2,1)S(1)} collective-permute-done((bf16[128,2048]{1,0:T(8,128)(2,1)}, bf16[128,2048]{1,0:T(8,128)(2,1)S(1)}, u32[]{:S(2)}, u32[]{:S(2)}) %collective-permute-start) | collective-permute-done | bytes 524320 | tf_op jit(solution)/shard_map/gather/ppermute | solution.py:493
  18.8 0.0 collective-permute-start.2
  18.8 0.7 pad_add_fusion.at
  19.5 3.9 %spread_input.1 = (bf16[8,128,256]{2,1,0:T(8,128)(2,1)}, bf16[8,128,256]{2,1,0:T(8,128)(2,1)}, bf16[8,128,256]{2,1,0:T(8,128)(2,1)}, bf16[8,128,256]{2,1,0:T(8,128)(2,1)}) custom-call(s32[2]{0:T(128)} %pad_add_fusion.at, bf16[128,8192]{1,0:T(8,128)(2,1)} %x), custom_call_target="tpu_custom_call" | custom-call | tf_op jit(solution)/shard_map/spread_input/pallas_call | solution.py:362
  23.4 3.1 %collective-permute-start.3 = (bf16[8,128,256]{2,1,0:T(8,128)(2,1)}, bf16[8,128,256]{2,1,0:T(8,128)(2,1)S(1)}, u32[]{:S(2)}, u32[]{:S(2)}) collective-permute-start(bf16[8,128,256]{2,1,0:T(8,128)(2,1)} %get-tuple-element.59), channel_id=1, source_target_pairs={{0,128},{128,0},{1,129},{129,1},{2,130},{130,2},{3,131},{131,3},{4... | collective-permute-start | bytes 1572872 | tf_op jit(solution)/shard_map/spread_input/ppermute | solution.py:493
  26.5 0.2 collective-permute-start.4
  26.6 0.5 collective-permute-start.5
  27.1 0.6 stack.60.where
  27.7 4.4 %all-to-all-done.packed = bf16[8,128,256]{2,1,0:T(8,128)(2,1)S(1)} async-done(((bf16[8,128,256]{2,1,0:T(8,128)(2,1)}), bf16[8,128,256]{2,1,0:T(8,128)(2,1)S(1)}, u32[]{:S(2)}, u32[]{:S(2)}) %all-to-all-start) | async-done | bytes 524320 | tf_op jit(solution)/shard_map/gather/all_to_all | solution.py:525
  32.1 0.0 collective-permute-done.1.side
  32.1 0.0 collective-permute-done.2.both
  32.1 0.8 copy-done.3
  32.9 0.2 copy-done.6
  33.1 10.8 %attention_stats.1.s_own = f32[3,8,512]{2,1,0:T(8,128)} custom-call(s32[64]{0:T(128)} %order.3, s32[12]{0:T(128)} %stack.60.where, bf16[128,2048]{1,0:T(8,128)(2,1)} %get-tuple-element.50.own, bf16[128,2048]{1,0:T(8,128)(2,1)} %copy-done.5, bf16[128,2048]{1,0:T(8,128)(2,1)} %copy-done.6, bf16[128,2048]{1,0:T(8,128)(2,1)} %collective-permute-done.2.both, ...), custom_call_target="tpu_custom_call" | custom-call | flops 1073741824 | bytes 8388608 | tf_op jit(solution)/shard_map/attention_stats/pallas_call | solution.py:276
  43.9 0.0 collective-permute-done.3.x1
  43.9 0.0 collective-permute-done.4.x2
  44.0 6.2 %collective-permute-done.5.x3 = bf16[8,128,256]{2,1,0:T(8,128)(2,1)S(1)} collective-permute-done((bf16[8,128,256]{2,1,0:T(8,128)(2,1)}, bf16[8,128,256]{2,1,0:T(8,128)(2,1)S(1)}, u32[]{:S(2)}, u32[]{:S(2)}) %collective-permute-start.5) | collective-permute-done | bytes 524320 | tf_op jit(solution)/shard_map/spread_input/ppermute | solution.py:497
  50.2 2.9 %collective-permute-start.8 = (f32[3,8,512]{2,1,0:T(8,128)}, f32[3,8,512]{2,1,0:T(8,128)S(1)}, u32[]{:S(2)}, u32[]{:S(2)}) collective-permute-start(f32[3,8,512]{2,1,0:T(8,128)} %attention_stats.1.s_own), channel_id=1, source_target_pairs={{0,136},{8,128},{128,8},{136,0},{1,137},{9,129},{129,9},{137,1},{2... | collective-permute-start | bytes 147464 | tf_op jit(solution)/shard_map/share_stats/ppermute | solution.py:497
  53.1 0.2 collective-permute-start.7
  53.3 0.5 collective-permute-start.6
  53.8 1.7 %collective-permute-done.8.s_both = f32[3,8,512]{2,1,0:T(8,128)S(1)} collective-permute-done((f32[3,8,512]{2,1,0:T(8,128)}, f32[3,8,512]{2,1,0:T(8,128)S(1)}, u32[]{:S(2)}, u32[]{:S(2)}) %collective-permute-start.8) | collective-permute-done | bytes 49184 | tf_op jit(solution)/shard_map/share_stats/ppermute | solution.py:497
  55.6 0.0 collective-permute-done.7.s_side
  55.6 3.6 %collective-permute-done.6.s_far = f32[3,8,512]{2,1,0:T(8,128)S(1)} collective-permute-done((f32[3,8,512]{2,1,0:T(8,128)}, f32[3,8,512]{2,1,0:T(8,128)S(1)}, u32[]{:S(2)}, u32[]{:S(2)}) %collective-permute-start.6) | collective-permute-done | bytes 49184 | tf_op jit(solution)/shard_map/share_stats/ppermute | solution.py:493
  59.1 0.6 copy-done.9
  59.8 13.3 %attention_grads.1 = (f32[128,1024]{1,0:T(8,128)}, f32[128,1024]{1,0:T(8,128)}, bf16[2,128,1024]{2,1,0:T(8,128)(2,1)}, bf16[8,128,256]{2,1,0:T(8,128)(2,1)}) custom-call(s32[64]{0:T(128)} %order.3, s32[12]{0:T(128)} %stack.60.where, bf16[128,2048]{1,0:T(8,128)(2,1)} %get-tuple-element.50.own, bf16[128,2048]{1,0:T(8,128)(2,1)} %copy-done.5, ...), custom_call_target="tpu_custom_call" | custom-call | flops 2684354560 | bytes 8388608 | tf_op jit(solution)/shard_map/attention_grads/pallas_call | solution.py:293
  73.1 0.3 collective-permute-start.9
  73.4 8.1 %all-to-all-start.1 = ((bf16[8,128,256]{2,1,0:T(8,128)(2,1)}), bf16[8,128,256]{2,1,0:T(8,128)(2,1)S(1)}, u32[]{:S(2)}, u32[]{:S(2)}) async-start(bf16[8,128,256]{2,1,0:T(8,128)(2,1)} %get-tuple-element.63), calls=%async_computation.1 | async-start | bytes 1048576 | tf_op jit(solution)/shard_map/scatter_grads/all_to_all | solution.py:545
  81.5 0.0 collective-permute-done.9
  81.5 0.1 convert_element_type.14
  81.7 1.2 fusion.1
  82.8 1.1 collective-permute-start.10
  84.0 8.7 %collective-permute-done.10 = bf16[128,1024]{1,0:T(8,128)(2,1)S(1)} collective-permute-done((bf16[128,1024]{1,0:T(8,128)(2,1)S(1)}, bf16[128,1024]{1,0:T(8,128)(2,1)S(1)}, u32[]{:S(2)}, u32[]{:S(2)}) %collective-permute-start.10) | collective-permute-done | bytes 262176 | tf_op jit(solution)/shard_map/query_grads/ppermute | solution.py:493
  92.7 6.8 %all-to-all-done.1.parts = bf16[8,128,256]{2,1,0:T(8,128)(2,1)S(1)} async-done(((bf16[8,128,256]{2,1,0:T(8,128)(2,1)}), bf16[8,128,256]{2,1,0:T(8,128)(2,1)S(1)}, u32[]{:S(2)}, u32[]{:S(2)}) %all-to-all-start.1) | async-done | bytes 524320 | tf_op jit(solution)/shard_map/scatter_grads/all_to_all | solution.py:545
  99.5 0.1 scatter_grads.1.grad.g0
  99.6 0.0 copy-start
  99.6 0.6 collective-permute-start.13
  100.2 0.5 collective-permute-start.12
  100.7 2.6 %collective-permute-start.11 = (bf16[128,256]{1,0:T(8,128)(2,1)S(1)}, bf16[128,256]{1,0:T(8,128)(2,1)S(1)}, u32[]{:S(2)}, u32[]{:S(2)}) collective-permute-start(bf16[128,256]{1,0:T(8,128)(2,1)S(1)} %scatter_grads.1.grad.g0), channel_id=1, source_target_pairs={{0,128},{128,0},{1,129},{129,1},{2,130},{130,2},{3,131},{131,3},{4... | collective-permute-start | bytes 196616 | tf_op jit(solution)/shard_map/scatter_grads/ppermute | solution.py:493
  103.4 5.8 %input_grad.1 = bf16[8,128,1024]{2,1,0:T(8,128)(2,1)} custom-call(bf16[128,256]{1,0:T(8,128)(2,1)} %copy-done, bf16[8192,128]{1,0:T(8,128)(2,1)} %key_weight.1, bf16[8192,128]{1,0:T(8,128)(2,1)} %value_weight.1), custom_call_target="tpu_custom_call" | custom-call | flops 536870912 | bytes 6291456 | tf_op jit(solution)/shard_map/input_grad/pallas_call | solution.py:412
  109.1 0.0 copy-start.1
  109.2 0.0 collective-permute-done.11.g1
  109.2 4.8 %all-to-all-start.2 = ((bf16[8,128,1024]{2,1,0:T(8,128)(2,1)}), bf16[8,128,1024]{2,1,0:T(8,128)(2,1)}, u32[]{:S(2)}, u32[]{:S(2)}) async-start(bf16[8,128,1024]{2,1,0:T(8,128)(2,1)} %input_grad.1), calls=%async_computation.2 | async-start | bytes 4194304 | tf_op jit(solution)/shard_map/input_grad/all_to_all | solution.py:563
  114.0 1.5 %weight_grad.2 = (f32[256,256]{1,0:T(8,128)S(1)}, bf16[256,256]{1,0:T(8,128)(2,1)S(1)}, bf16[256,256]{1,0:T(8,128)(2,1)S(1)}, bf16[256,256]{1,0:T(8,128)(2,1)S(1...) custom-call(s32[1]{0:T(128)} %bitcast.16.at, ...), custom_call_target="tpu_custom_call" | custom-call | flops 536870912 | bytes 4194304 | tf_op jit(solution)/shard_map/weight_grad/pallas_call | solution.py:455
  115.6 0.6 collective-permute-start.14
  116.2 0.1 add_convert_fusion
  116.3 2.8 %collective-permute-start.16 = (bf16[256,256]{1,0:T(8,128)(2,1)S(1)}, bf16[256,256]{1,0:T(8,128)(2,1)S(1)}, u32[]{:S(2)}, u32[]{:S(2)}) collective-permute-start(bf16[256,256]{1,0:T(8,128)(2,1)S(1)} %get-tuple-element.82), channel_id=1, source_target_pairs={{0,48},{16,64},{32,80},{48,96},{64,112},{80,0},{96,16},{112,32},{1... | collective-permute-start | bytes 393224 | tf_op jit(solution)/shard_map/weight_grad/ppermute | solution.py:569
  119.1 3.3 %collective-permute-start.17 = (bf16[256,256]{1,0:T(8,128)(2,1)S(1)}, bf16[256,256]{1,0:T(8,128)(2,1)S(1)}, u32[]{:S(2)}, u32[]{:S(2)}) collective-permute-start(bf16[256,256]{1,0:T(8,128)(2,1)S(1)} %get-tuple-element.83), channel_id=1, source_target_pairs={{0,64},{16,80},{32,96},{48,112},{64,0},{80,16},{96,32},{112,48},{1... | collective-permute-start | bytes 393224 | tf_op jit(solution)/shard_map/weight_grad/ppermute | solution.py:569
  122.4 1.3 collective-permute-start.18
  123.7 2.3 %collective-permute-done.14.refs_1_ = bf16[256,256]{1,0:T(8,128)(2,1)S(1)} collective-permute-done((bf16[256,256]{1,0:T(8,128)(2,1)S(1)}, bf16[256,256]{1,0:T(8,128)(2,1)S(1)}, u32[]{:S(2)}, u32[]{:S(2)}) %collective-permute-start.14) | collective-permute-done | bytes 131104 | tf_op jit(solution)/shard_map/weight_grad/ppermute | solution.py:569
  126.0 1.0 collective-permute-start.19
  127.0 5.0 %collective-permute-done.15.refs_2_ = bf16[256,256]{1,0:T(8,128)(2,1)S(1)} collective-permute-done((bf16[256,256]{1,0:T(8,128)(2,1)S(1)}, bf16[256,256]{1,0:T(8,128)(2,1)S(1)}, u32[]{:S(2)}, u32[]{:S(2)}) %collective-permute-start.15) | collective-permute-done | bytes 131104 | tf_op jit(solution)/shard_map/weight_grad/ppermute | solution.py:569
  132.0 1.3 collective-permute-start.20
  133.3 0.7 fusion.3
  134.0 3.4 %collective-permute-done.16.refs_3_ = bf16[256,256]{1,0:T(8,128)(2,1)S(1)} collective-permute-done((bf16[256,256]{1,0:T(8,128)(2,1)S(1)}, bf16[256,256]{1,0:T(8,128)(2,1)S(1)}, u32[]{:S(2)}, u32[]{:S(2)}) %collective-permute-start.16) | collective-permute-done | bytes 131104 | tf_op jit(solution)/shard_map/weight_grad/ppermute | solution.py:569
  137.4 0.3 collective-permute-done.18.refs_5_
  137.6 6.6 %collective-permute-done.19.refs_6_ = bf16[256,256]{1,0:T(8,128)(2,1)S(1)} collective-permute-done((bf16[256,256]{1,0:T(8,128)(2,1)S(1)}, bf16[256,256]{1,0:T(8,128)(2,1)S(1)}, u32[]{:S(2)}, u32[]{:S(2)}) %collective-permute-start.19) | collective-permute-done | bytes 131104 | tf_op jit(solution)/shard_map/weight_grad/ppermute | solution.py:569
  144.2 0.7 collective-permute-done.20.refs_7_
  145.0 0.8 weight_grad.3
  145.8 0.0 all-to-all-done.2
  145.8 2.7 %reduce_sum.12 = bf16[128,1024]{1,0:T(8,128)(2,1)} reduce(bf16[8,128,1024]{2,1,0:T(8,128)(2,1)} %all-to-all-done.2, bf16[]{:T(256)} %constant.34.clone.1), dimensions={0}, to_apply=%region_0.0 | reduce | flops 917504 | bytes 2359298 | tf_op jit(solution)/shard_map/input_grad/reduce_sum | solution.py:564
  (19 shorter events, 0.0 us)
Async XLA Ops:
  3.3 15.5 %collective-permute-start = (bf16[128,2048]{1,0:T(8,128)(2,1)}, bf16[128,2048]{1,0:T(8,128)(2,1)S(1)}, u32[]{:S(2)}, u32[]{:S(2)}) collective-permute-start(bf16[128,2048]{1,0:T(8,128)(2,1)} %get-tuple-element.50.own), channel_id=1, source_target_pairs={{0,128},{128,0},{1,129},{129,1},{2,130},{130,2},{3,131},{131,3},{4... | collective-permute-start | bytes 1572872 | tf_op jit(solution)/shard_map/gather/ppermute | solution.py:493
  6.4 25.7 %all-to-all-start = ((bf16[8,128,256]{2,1,0:T(8,128)(2,1)}), bf16[8,128,256]{2,1,0:T(8,128)(2,1)S(1)}, u32[]{:S(2)}, u32[]{:S(2)}) async-start(bf16[8,128,256]{2,1,0:T(8,128)(2,1)} %get-tuple-element.47), calls=%async_computation | async-start | bytes 1048576 | tf_op jit(solution)/shard_map/gather/all_to_all | solution.py:525
  14.9 17.2 %collective-permute-start.1 = (bf16[128,2048]{1,0:T(8,128)(2,1)}, bf16[128,2048]{1,0:T(8,128)(2,1)S(1)}, u32[]{:S(2)}, u32[]{:S(2)}) collective-permute-start(bf16[128,2048]{1,0:T(8,128)(2,1)} %get-tuple-element.50.own), channel_id=1, source_target_pairs={{0,8},{8,0},{1,9},{9,1},{2,10},{10,2},{3,11},{11,3},{4,12},{12,4},... | collective-permute-start | bytes 1572872 | tf_op jit(solution)/shard_map/gather/ppermute | solution.py:493
  18.8 13.3 %copy-start.5 = (bf16[128,2048]{1,0:T(8,128)(2,1)}, bf16[128,2048]{1,0:T(8,128)(2,1)S(1)}, u32[]{:S(2)}) copy-start(bf16[128,2048]{1,0:T(8,128)(2,1)S(1)} %collective-permute-done.far) | copy-start | bytes 1572868
  18.8 13.3 %collective-permute-start.2 = (bf16[128,2048]{1,0:T(8,128)(2,1)S(1)}, bf16[128,2048]{1,0:T(8,128)(2,1)}, u32[]{:S(2)}, u32[]{:S(2)}) collective-permute-start(bf16[128,2048]{1,0:T(8,128)(2,1)S(1)} %collective-permute-done.far), channel_id=1, source_target_pairs={{0,8},{8,0},{1,9},{9,1},{2,10},{10,2},{3,11},{11,3},{4,12},{12,4},... | collective-permute-start | bytes 1572872 | tf_op jit(solution)/shard_map/gather/ppermute | solution.py:493
  23.4 20.6 %collective-permute-start.3 = (bf16[8,128,256]{2,1,0:T(8,128)(2,1)}, bf16[8,128,256]{2,1,0:T(8,128)(2,1)S(1)}, u32[]{:S(2)}, u32[]{:S(2)}) collective-permute-start(bf16[8,128,256]{2,1,0:T(8,128)(2,1)} %get-tuple-element.59), channel_id=1, source_target_pairs={{0,128},{128,0},{1,129},{129,1},{2,130},{130,2},{3,131},{131,3},{4... | collective-permute-start | bytes 1572872 | tf_op jit(solution)/shard_map/spread_input/ppermute | solution.py:493
  26.5 17.5 %collective-permute-start.4 = (bf16[8,128,256]{2,1,0:T(8,128)(2,1)}, bf16[8,128,256]{2,1,0:T(8,128)(2,1)S(1)}, u32[]{:S(2)}, u32[]{:S(2)}) collective-permute-start(bf16[8,128,256]{2,1,0:T(8,128)(2,1)} %get-tuple-element.60), channel_id=1, source_target_pairs={{0,8},{8,0},{1,9},{9,1},{2,10},{10,2},{3,11},{11,3},{4,12},{12,4},... | collective-permute-start | bytes 1572872 | tf_op jit(solution)/shard_map/spread_input/ppermute | solution.py:493
  26.6 23.6 %collective-permute-start.5 = (bf16[8,128,256]{2,1,0:T(8,128)(2,1)}, bf16[8,128,256]{2,1,0:T(8,128)(2,1)S(1)}, u32[]{:S(2)}, u32[]{:S(2)}) collective-permute-start(bf16[8,128,256]{2,1,0:T(8,128)(2,1)} %get-tuple-element.61), channel_id=1, source_target_pairs={{0,136},{8,128},{128,8},{136,0},{1,137},{9,129},{129,9},{137,1},{2... | collective-permute-start | bytes 1572872 | tf_op jit(solution)/shard_map/spread_input/ppermute | solution.py:497
  32.1 0.8 copy-start.3
  32.1 1.0 copy-start.6
  50.2 5.4 %collective-permute-start.8 = (f32[3,8,512]{2,1,0:T(8,128)}, f32[3,8,512]{2,1,0:T(8,128)S(1)}, u32[]{:S(2)}, u32[]{:S(2)}) collective-permute-start(f32[3,8,512]{2,1,0:T(8,128)} %attention_stats.1.s_own), channel_id=1, source_target_pairs={{0,136},{8,128},{128,8},{136,0},{1,137},{9,129},{129,9},{137,1},{2... | collective-permute-start | bytes 147464 | tf_op jit(solution)/shard_map/share_stats/ppermute | solution.py:497
  53.1 2.4 %collective-permute-start.7 = (f32[3,8,512]{2,1,0:T(8,128)}, f32[3,8,512]{2,1,0:T(8,128)S(1)}, u32[]{:S(2)}, u32[]{:S(2)}) collective-permute-start(f32[3,8,512]{2,1,0:T(8,128)} %attention_stats.1.s_own), channel_id=1, source_target_pairs={{0,8},{8,0},{1,9},{9,1},{2,10},{10,2},{3,11},{11,3},{4,12},{12,4},... | collective-permute-start | bytes 147464 | tf_op jit(solution)/shard_map/share_stats/ppermute | solution.py:493
  53.3 5.8 %collective-permute-start.6 = (f32[3,8,512]{2,1,0:T(8,128)}, f32[3,8,512]{2,1,0:T(8,128)S(1)}, u32[]{:S(2)}, u32[]{:S(2)}) collective-permute-start(f32[3,8,512]{2,1,0:T(8,128)} %attention_stats.1.s_own), channel_id=1, source_target_pairs={{0,128},{128,0},{1,129},{129,1},{2,130},{130,2},{3,131},{131,3},{4... | collective-permute-start | bytes 147464 | tf_op jit(solution)/shard_map/share_stats/ppermute | solution.py:493
  55.6 3.6 %copy-start.7 = (f32[3,8,512]{2,1,0:T(8,128)}, f32[3,8,512]{2,1,0:T(8,128)S(1)}, u32[]{:S(2)}) copy-start(f32[3,8,512]{2,1,0:T(8,128)S(1)} %collective-permute-done.8.s_both) | copy-start | bytes 147460
  55.6 3.6 %copy-start.8 = (f32[3,8,512]{2,1,0:T(8,128)}, f32[3,8,512]{2,1,0:T(8,128)S(1)}, u32[]{:S(2)}) copy-start(f32[3,8,512]{2,1,0:T(8,128)S(1)} %collective-permute-done.7.s_side) | copy-start | bytes 147460
  59.1 0.6 copy-start.9
  73.1 8.6 %copy-start.4 = (f32[128,1024]{1,0:T(8,128)S(1)}, f32[128,1024]{1,0:T(8,128)}, u32[]{:S(2)}) copy-start(f32[128,1024]{1,0:T(8,128)} %get-tuple-element.64) | copy-start | bytes 1572868
  73.1 8.4 %collective-permute-start.9 = (bf16[2,128,1024]{2,1,0:T(8,128)(2,1)}, bf16[2,128,1024]{2,1,0:T(8,128)(2,1)S(1)}, u32[]{:S(2)}, u32[]{:S(2)}) collective-permute-start(bf16[2,128,1024]{2,1,0:T(8,128)(2,1)} %get-tuple-element.65), channel_id=1, source_target_pairs={{0,8},{8,0},{1,9},{9,1},{2,10},{10,2},{3,11},{11,3},{4,12},{12,4},... | collective-permute-start | bytes 1572872 | tf_op jit(solution)/shard_map/query_grads/ppermute | solution.py:493
  73.4 26.1 %all-to-all-start.1 = ((bf16[8,128,256]{2,1,0:T(8,128)(2,1)}), bf16[8,128,256]{2,1,0:T(8,128)(2,1)S(1)}, u32[]{:S(2)}, u32[]{:S(2)}) async-start(bf16[8,128,256]{2,1,0:T(8,128)(2,1)} %get-tuple-element.63), calls=%async_computation.1 | async-start | bytes 1048576 | tf_op jit(solution)/shard_map/scatter_grads/all_to_all | solution.py:545
  82.8 9.9 %collective-permute-start.10 = (bf16[128,1024]{1,0:T(8,128)(2,1)S(1)}, bf16[128,1024]{1,0:T(8,128)(2,1)S(1)}, u32[]{:S(2)}, u32[]{:S(2)}) collective-permute-start(bf16[128,1024]{1,0:T(8,128)(2,1)S(1)} %get-tuple-element.89), channel_id=1, source_target_pairs={{0,128},{128,0},{1,129},{129,1},{2,130},{130,2},{3,131},{131,3},{4... | collective-permute-start | bytes 786440 | tf_op jit(solution)/shard_map/query_grads/ppermute | solution.py:493
  99.6 3.7 %copy-start = (bf16[128,256]{1,0:T(8,128)(2,1)}, bf16[128,256]{1,0:T(8,128)(2,1)S(1)}, u32[]{:S(2)}) copy-start(bf16[128,256]{1,0:T(8,128)(2,1)S(1)} %scatter_grads.1.grad.g0) | copy-start | bytes 196612
  99.6 9.5 %collective-permute-start.13 = (bf16[128,256]{1,0:T(8,128)(2,1)S(1)}, bf16[128,256]{1,0:T(8,128)(2,1)S(1)}, u32[]{:S(2)}, u32[]{:S(2)}) collective-permute-start(bf16[128,256]{1,0:T(8,128)(2,1)S(1)} %scatter_grads.1.grad.g0), channel_id=1, source_target_pairs={{0,136},{8,128},{128,8},{136,0},{1,137},{9,129},{129,9},{137,1},{2... | collective-permute-start | bytes 196616 | tf_op jit(solution)/shard_map/scatter_grads/ppermute | solution.py:497
  100.2 8.9 %collective-permute-start.12 = (bf16[128,256]{1,0:T(8,128)(2,1)S(1)}, bf16[128,256]{1,0:T(8,128)(2,1)S(1)}, u32[]{:S(2)}, u32[]{:S(2)}) collective-permute-start(bf16[128,256]{1,0:T(8,128)(2,1)S(1)} %scatter_grads.1.grad.g0), channel_id=1, source_target_pairs={{0,8},{8,0},{1,9},{9,1},{2,10},{10,2},{3,11},{11,3},{4,12},{12,4},... | collective-permute-start | bytes 196616 | tf_op jit(solution)/shard_map/scatter_grads/ppermute | solution.py:493
  100.7 8.5 %collective-permute-start.11 = (bf16[128,256]{1,0:T(8,128)(2,1)S(1)}, bf16[128,256]{1,0:T(8,128)(2,1)S(1)}, u32[]{:S(2)}, u32[]{:S(2)}) collective-permute-start(bf16[128,256]{1,0:T(8,128)(2,1)S(1)} %scatter_grads.1.grad.g0), channel_id=1, source_target_pairs={{0,128},{128,0},{1,129},{129,1},{2,130},{130,2},{3,131},{131,3},{4... | collective-permute-start | bytes 196616 | tf_op jit(solution)/shard_map/scatter_grads/ppermute | solution.py:493
  109.1 4.9 %copy-start.1 = (bf16[128,256]{1,0:T(8,128)(2,1)S(1)}, bf16[128,256]{1,0:T(8,128)(2,1)}, u32[]{:S(2)}) copy-start(bf16[128,256]{1,0:T(8,128)(2,1)} %copy-done) | copy-start | bytes 196612
  109.1 4.9 %copy-start.2 = (bf16[8,128,256]{2,1,0:T(8,128)(2,1)S(1)}, bf16[8,128,256]{2,1,0:T(8,128)(2,1)}, u32[]{:S(2)}) copy-start(bf16[8,128,256]{2,1,0:T(8,128)(2,1)} %get-tuple-element.75.x0) | copy-start | bytes 1572868
  109.2 36.6 %all-to-all-start.2 = ((bf16[8,128,1024]{2,1,0:T(8,128)(2,1)}), bf16[8,128,1024]{2,1,0:T(8,128)(2,1)}, u32[]{:S(2)}, u32[]{:S(2)}) async-start(bf16[8,128,1024]{2,1,0:T(8,128)(2,1)} %input_grad.1), calls=%async_computation.2 | async-start | bytes 4194304 | tf_op jit(solution)/shard_map/input_grad/all_to_all | solution.py:563
  115.6 10.4 %collective-permute-start.14 = (bf16[256,256]{1,0:T(8,128)(2,1)S(1)}, bf16[256,256]{1,0:T(8,128)(2,1)S(1)}, u32[]{:S(2)}, u32[]{:S(2)}) collective-permute-start(bf16[256,256]{1,0:T(8,128)(2,1)S(1)} %get-tuple-element.80), channel_id=1, source_target_pairs={{0,16},{16,32},{32,48},{48,64},{64,80},{80,96},{96,112},{112,0},{1... | collective-permute-start | bytes 393224 | tf_op jit(solution)/shard_map/weight_grad/ppermute | solution.py:569
  116.2 15.8 %collective-permute-start.15 = (bf16[256,256]{1,0:T(8,128)(2,1)S(1)}, bf16[256,256]{1,0:T(8,128)(2,1)S(1)}, u32[]{:S(2)}, u32[]{:S(2)}) collective-permute-start(bf16[256,256]{1,0:T(8,128)(2,1)S(1)} %get-tuple-element.81), channel_id=1, source_target_pairs={{0,32},{16,48},{32,64},{48,80},{64,96},{80,112},{96,0},{112,16},{1... | collective-permute-start | bytes 393224 | tf_op jit(solution)/shard_map/weight_grad/ppermute | solution.py:569
  116.3 21.1 %collective-permute-start.16 = (bf16[256,256]{1,0:T(8,128)(2,1)S(1)}, bf16[256,256]{1,0:T(8,128)(2,1)S(1)}, u32[]{:S(2)}, u32[]{:S(2)}) collective-permute-start(bf16[256,256]{1,0:T(8,128)(2,1)S(1)} %get-tuple-element.82), channel_id=1, source_target_pairs={{0,48},{16,64},{32,80},{48,96},{64,112},{80,0},{96,16},{112,32},{1... | collective-permute-start | bytes 393224 | tf_op jit(solution)/shard_map/weight_grad/ppermute | solution.py:569
  119.1 18.2 %collective-permute-start.17 = (bf16[256,256]{1,0:T(8,128)(2,1)S(1)}, bf16[256,256]{1,0:T(8,128)(2,1)S(1)}, u32[]{:S(2)}, u32[]{:S(2)}) collective-permute-start(bf16[256,256]{1,0:T(8,128)(2,1)S(1)} %get-tuple-element.83), channel_id=1, source_target_pairs={{0,64},{16,80},{32,96},{48,112},{64,0},{80,16},{96,32},{112,48},{1... | collective-permute-start | bytes 393224 | tf_op jit(solution)/shard_map/weight_grad/ppermute | solution.py:569
  122.4 15.2 %collective-permute-start.18 = (bf16[256,256]{1,0:T(8,128)(2,1)S(1)}, bf16[256,256]{1,0:T(8,128)(2,1)S(1)}, u32[]{:S(2)}, u32[]{:S(2)}) collective-permute-start(bf16[256,256]{1,0:T(8,128)(2,1)S(1)} %get-tuple-element.84), channel_id=1, source_target_pairs={{0,80},{16,96},{32,112},{48,0},{64,16},{80,32},{96,48},{112,64},{1... | collective-permute-start | bytes 393224 | tf_op jit(solution)/shard_map/weight_grad/ppermute | solution.py:569
  126.0 18.2 %collective-permute-start.19 = (bf16[256,256]{1,0:T(8,128)(2,1)S(1)}, bf16[256,256]{1,0:T(8,128)(2,1)S(1)}, u32[]{:S(2)}, u32[]{:S(2)}) collective-permute-start(bf16[256,256]{1,0:T(8,128)(2,1)S(1)} %get-tuple-element.85), channel_id=1, source_target_pairs={{0,96},{16,112},{32,0},{48,16},{64,32},{80,48},{96,64},{112,80},{1... | collective-permute-start | bytes 393224 | tf_op jit(solution)/shard_map/weight_grad/ppermute | solution.py:569
  132.0 13.0 %collective-permute-start.20 = (bf16[256,256]{1,0:T(8,128)(2,1)S(1)}, bf16[256,256]{1,0:T(8,128)(2,1)S(1)}, u32[]{:S(2)}, u32[]{:S(2)}) collective-permute-start(bf16[256,256]{1,0:T(8,128)(2,1)S(1)} %get-tuple-element.86), channel_id=1, source_target_pairs={{0,112},{16,0},{32,16},{48,32},{64,48},{80,64},{96,80},{112,96},{1... | collective-permute-start | bytes 393224 | tf_op jit(solution)/shard_map/weight_grad/ppermute | solution.py:569

commit v2 on v1

--- a/solution.py
+++ b/solution.py
@@ -23,7 +23,6 @@
 TO_LOG2 = SCALE * math.log2(math.e)
 LOWEST = -1e30
 BIG = 56 * 2**20
-MIDDLE = 16 * 2**20
 SMALL = 8 * 2**20
 VMEM = pl.BlockSpec(memory_space=pltpu.VMEM)
 SMEM = pl.BlockSpec(memory_space=pltpu.SMEM)
@@ -131,24 +130,23 @@
 
 
 def stats_kernel(
-    order, where, own, far, side, both, packed, stats, held, kv_held, k_sorted, v_sorted, q_all, g_all, sems,
-    scores, peak, total, delta,
+    order, where, own, far, side, both, kv, stats, k_out, v_out, q_out, g_out, held, k_sorted, v_sorted, q_all, g_all,
+    sems, out_sems, scores, peak, total, delta,
 ):
     half = own.shape[0] // 2
-    n_keys = packed.shape[0]
-    width = q_all.shape[1]
-    copies = fetch(
-        [(packed, kv_held)] + [(ref, held.at[a]) for a, ref in enumerate((own, far, side, both))], sems
-    )
+    n_keys = kv.shape[0]
+    width = q_all.shape[2]
+    copies = fetch([(ref, held.at[a]) for a, ref in enumerate((own, far, side, both))], sems)
     plan = Plan(order, where, n_keys, half)
-    copies[0].wait()
-    sort_keys(plan, kv_held, k_sorted, v_sorted)
+    sort_keys(plan, kv, k_sorted, v_sorted)
+    sent = fetch([(k_sorted, k_out), (v_sorted, v_out)], out_sems.at[0])
     for a in range(4):
-        copies[1 + a].wait()
-        load_heads(a, held.at[a], q_all, g_all, order, where, half)
+        copies[a].wait()
+        load_heads(a, held.at[a], q_all.at[a], g_all.at[a], order, where, half)
+        sent += fetch([(q_all.at[a], q_out.at[a]), (g_all.at[a], g_out.at[a])], out_sems.at[1 + a])
         early, late, last_early, last_late = plan.limits(a, width)
         for part, seen, last in ((0, late, last_late), (1, early, last_early)):
-            q, g = q_all[part], g_all[part]
+            q, g = q_all[a, part], g_all[a, part]
             peak[...] = jnp.full(peak.shape, LOWEST, f32)
             for start, size, condition, masked in tiles(seen, n_keys, half, part):
 
@@ -176,38 +174,36 @@
             stats[0, row:row + 1, :] = top
             stats[1, row:row + 1, :] = jnp.sum(total[...], axis=0, keepdims=True)
             stats[2, row:row + 1, :] = jnp.sum(delta[...], axis=0, keepdims=True)
+    for copy in sent:
+        copy.wait()
 
 
 def grads_kernel(
-    order, where, own, far, side, both, packed, s_own, s_far, s_side, s_both, dq_own, dq_far, dq_pair, dkv,
-    held, kv_held, k_sorted, v_sorted, q_all, g_all, sems, s_held, out_mine, out_pair, out_kv, out_sems, dk, dv, dq,
+    order, where, keys, values, queries, grads, s_own, s_far, s_side, s_both, dq_own, dq_far, dq_pair, dkv,
+    k_sorted, v_sorted, q_all, g_all, sems, s_held, out_mine, out_pair, out_kv, out_sems, dk, dv, dq,
 ):
-    half = own.shape[0] // 2
-    n_keys = packed.shape[0]
-    width = q_all.shape[1]
-    copies = fetch(
-        [(packed, kv_held)]
-        + [(ref, held.at[a]) for a, ref in enumerate((own, far, side, both))]
-        + [(ref, s_held.at[a]) for a, ref in enumerate((s_own, s_far, s_side, s_both))],
-        sems,
-    )
+    n_keys, half = dkv.shape[0], dkv.shape[1] // 2
+    width = q_all.shape[2]
+    copies = fetch([(keys, k_sorted), (values, v_sorted)], sems.at[0])
+    parts = [
+        fetch([(queries.at[a], q_all.at[a]), (grads.at[a], g_all.at[a])], sems.at[1 + a]) for a in range(4)
+    ]
+    copies += fetch([(ref, s_held.at[a]) for a, ref in enumerate((s_own, s_far, s_side, s_both))], sems.at[5])
     plan = Plan(order, where, n_keys, half)
-    copies[0].wait()
-    sort_keys(plan, kv_held, k_sorted, v_sorted)
     dk[...] = jnp.zeros(dk.shape, f32)
     dv[...] = jnp.zeros(dv.shape, f32)
-    for copy in copies[5:9]:
+    for copy in copies:
         copy.wait()
     sent = []
     for a, out in enumerate((dq_own, dq_far, dq_pair.at[0], dq_pair.at[1])):
         dq_out = out_pair.at[a - 2] if a > 1 else out_mine.at[a]
-        copies[1 + a].wait()
-        load_heads(a, held.at[a], q_all, g_all, order, where, half)
+        for copy in parts[a]:
+            copy.wait()
         early, late, last_early, last_late = plan.limits(a, width)
         slot = where[a]
         late_at = jnp.where(order[slot] > order[slot + 1], 0, 1)
         for part, seen, last, at in ((0, late, last_late, late_at), (1, early, last_early, 1 - late_at)):
-            q, g = q_all[part], g_all[part]
+            q, g = q_all[a, part], g_all[a, part]
             shares = []
             for flip in range(4):
                 r = 2 * (a ^ flip) + part
@@ -219,7 +215,7 @@
             dq[...] = jnp.zeros(dq.shape, f32)
             for start, size, condition, masked in tiles(seen, n_keys, half, part):
 
-                def grads():
+                def step():
                     span = slice(start, start + size)
                     k = k_sorted[span, :]
                     s = masked_scores(k, q, start, last, masked)
@@ -230,7 +226,7 @@
                     dk[span, :] += jnp.dot(ds, q, preferred_element_type=f32)
                     dq[...] += lax.dot_general(k, ds, TN, preferred_element_type=f32)
 
-                under(condition, grads)
+                under(condition, step)
             turned = (dq[...] * SCALE).T.astype(dq_out.dtype)
             rows = pl.ds(pl.multiple_of(at * half, half), half)
             for j in range(2 * GROUP):
@@ -250,16 +246,13 @@
         copy.wait()
 
 
-def scratch(n_keys, rows, copies):
+def scratch(n_keys, rows):
     width = GROUP * rows
     return [
-        pltpu.VMEM((4, rows, 4 * GROUP * DH), bf16),
-        pltpu.VMEM((n_keys, rows, 2 * DH), bf16),
         pltpu.VMEM((n_keys * rows, DH), bf16),
         pltpu.VMEM((n_keys * rows, DH), bf16),
-        pltpu.VMEM((2, width, DH), bf16),
-        pltpu.VMEM((2, width, DH), bf16),
-        pltpu.SemaphoreType.DMA((copies,)),
+        pltpu.VMEM((4, 2, width, DH), bf16),
+        pltpu.VMEM((4, 2, width, DH), bf16),
     ]
 
 
@@ -270,24 +263,28 @@
     )
 
 
-def attention_stats(order, where, own, far, side, both, packed):
-    n_keys, rows, _ = packed.shape
+def attention_stats(order, where, own, far, side, both, kv):
+    n_keys, rows, _ = kv.shape
     width = GROUP * rows
+    keys = jax.ShapeDtypeStruct((n_keys * rows, DH), bf16)
+    heads = jax.ShapeDtypeStruct((4, 2, width, DH), bf16)
     return pl.pallas_call(
         stats_kernel,
-        out_shape=jax.ShapeDtypeStruct((3, 8, width), f32),
-        in_specs=[SMEM] * 2 + [ANY] * 5,
-        out_specs=VMEM,
-        scratch_shapes=scratch(n_keys, rows, 5)
+        out_shape=(jax.ShapeDtypeStruct((3, 8, width), f32), keys, keys, heads, heads),
+        in_specs=[SMEM] * 2 + [ANY] * 4 + [VMEM],
+        out_specs=(VMEM,) + (ANY,) * 4,
+        scratch_shapes=[pltpu.VMEM((4,) + own.shape, bf16)]
+        + scratch(n_keys, rows)
+        + [pltpu.SemaphoreType.DMA((4,)), pltpu.SemaphoreType.DMA((5, 2))]
         + [pltpu.VMEM((n_keys * rows, width), f32)]
         + [pltpu.VMEM((8, width), f32)] * 3,
         compiler_params=pltpu.CompilerParams(vmem_limit_bytes=BIG),
         cost_estimate=cost(n_keys, rows, 2),
-    )(order, where, own, far, side, both, packed)
-
-
-def attention_grads(order, where, own, far, side, both, packed, stats):
-    n_keys, rows, _ = packed.shape
+    )(order, where, own, far, side, both, kv)
+
+
+def attention_grads(order, where, keys, values, queries, grads, stats, n_keys):
+    rows = keys.shape[0] // n_keys
     width = GROUP * rows
     shape = (rows, 2 * GROUP * DH)
     return pl.pallas_call(
@@ -298,10 +295,11 @@
             jax.ShapeDtypeStruct((2,) + shape, bf16),
             jax.ShapeDtypeStruct((n_keys, rows, 2 * DH), bf16),
         ),
-        in_specs=[SMEM] * 2 + [ANY] * 9,
+        in_specs=[SMEM] * 2 + [ANY] * 8,
         out_specs=(ANY,) * 4,
-        scratch_shapes=scratch(n_keys, rows, 9)
+        scratch_shapes=scratch(n_keys, rows)
         + [
+            pltpu.SemaphoreType.DMA((6, 4)),
             pltpu.VMEM((4, 3, 8, width), f32),
             pltpu.VMEM((2,) + shape, f32),
             pltpu.VMEM((2,) + shape, bf16),
@@ -312,7 +310,7 @@
         + [pltpu.VMEM((DH, width), f32)],
         compiler_params=pltpu.CompilerParams(vmem_limit_bytes=BIG),
         cost_estimate=cost(n_keys, rows, 5),
-    )(order, where, own, far, side, both, packed, *stats)
+    )(order, where, keys, values, queries, grads, *stats)
 
 
 def pack_kernel(*refs):
@@ -369,16 +367,16 @@
     )(at, x)
 
 
-def key_sum_kernel(parts, grad):
+def part_sum_kernel(parts, grad):
     total = parts[0].astype(f32)
     for i in range(1, parts.shape[0]):
         total += parts[i].astype(f32)
     grad[...] = total.astype(bf16)
 
 
-def key_sum(parts):
-    return pl.pallas_call(
-        key_sum_kernel,
+def part_sum(parts):
+    return pl.pallas_call(
+        part_sum_kernel,
         out_shape=jax.ShapeDtypeStruct(parts.shape[1:], bf16),
         in_specs=[VMEM],
         out_specs=VMEM,
@@ -462,7 +460,7 @@
             pltpu.VMEM((columns, 4 * rows), bf16),
             pltpu.SemaphoreType.DMA((4,)),
         ],
-        compiler_params=pltpu.CompilerParams(vmem_limit_bytes=MIDDLE),
+        compiler_params=pltpu.CompilerParams(vmem_limit_bytes=BIG),
         cost_estimate=pl.CostEstimate(
             flops=8 * rows * n_z * shape[0] * shape[1], bytes_accessed=4 * 2**20, transcendentals=0
         ),
@@ -525,21 +523,21 @@
         packed = lax.all_to_all(packed, "z", 0, 0)
         far = swap(own, "xh")
         side = swap(own, "core")
-        both = swap(far, "core")
         where, packed = lax.optimization_barrier((where, packed))
     with jax.named_scope("spread_input"):
         cuts = cut_input(at, shared_input, n_z)
         far, *cuts = lax.optimization_barrier((far, *cuts))
+        both = swap(far, "core")
         cuts = [cuts[0], swap(cuts[1], "xh"), swap(cuts[2], "core"), cross(cuts[3])]
 
     with jax.named_scope("attention_stats"):
-        stats = attention_stats(block_order, where, own, far, side, both, packed)
+        stats, *sorted_rows = attention_stats(block_order, where, own, far, side, both, packed)
     with jax.named_scope("share_stats"):
         stats, *cuts = lax.optimization_barrier((stats, *cuts))
         stats = (stats, swap(stats, "xh"), swap(stats, "core"), cross(stats))
     with jax.named_scope("attention_grads"):
         dq_own, dq_far, dq_pair, dkv = attention_grads(
-            block_order, where, own, far, side, both, packed, stats
+            block_order, where, *sorted_rows, stats, n_z
         )
     with jax.named_scope("scatter_grads"):
         dkv = lax.all_to_all(dkv, "z", 0, 0)
@@ -551,7 +549,7 @@
         dq = (dq_own + dq_far.astype(f32)).astype(bf16)
         dq_one, dq_two = dq[:, :GROUP * DH], dq[:, GROUP * DH:]
     with jax.named_scope("scatter_grads"):
-        grad = key_sum(dkv)
+        grad = part_sum(dkv)
 
         grads = [grad, swap(grad, "xh"), swap(grad, "core"), cross(grad)]
 
@@ -561,10 +559,11 @@
         terms = input_terms(grad, key_weight, value_weight, heads)
         terms, *grads = lax.optimization_barrier((terms, *grads))
         terms = lax.all_to_all(terms, HEAD, 0, 0)
-        input_grad = jnp.sum(terms.astype(f32), axis=0).astype(bf16)
+        input_grad = part_sum(terms)
 
     with jax.named_scope("weight_grad"):
         own, *rest = weight_terms(z.astype(jnp.int32).reshape(1), grads, cuts)
+        own, input_grad = lax.optimization_barrier((own, input_grad))
         parts = [own] + [
             lax.ppermute(part, "z", [(i, (i + k) % n_z) for i in range(n_z)])
             for k, part in enumerate(rest, 1)

time: 150 us -> 146 us (0.973)
  Pallas kernels: 38.9 us -> 43.8 us
  waiting for transfers between devices: 53.6 us -> 48.8 us
  other arithmetic: 4.73 us -> 0.91 us
    ppermute x3, waiting for transfers between devices: 7.96 us -> 2.57 us  [cross(): return lax.ppermute(x, ('xh', 'core'), [(0, 3), (1, 2), (2, 1), (3, 0)])]
    ppermute x11, waiting for transfers between devices: 16.2 us -> 12.3 us  [swap(): return lax.ppermute(x, axis, [(0, 1), (1, 0)])]
    all_to_all x1, waiting for transfers between devices: 4.41 us -> 7.81 us  [on_device(): packed = lax.all_to_all(packed, 'z', 0, 0)]
    pallas_call x1, Pallas kernels: 1.55 us -> 4.52 us  [weight_terms(): pl.pallas_call(weight_terms_kernel, out_shape=[jax.ShapeDtypeStruct(shape...]
    reduce_sum x1 -> x0, other arithmetic: 2.73 us -> none  [on_device(): input_grad = jnp.sum(terms.astype(f32), axis=0).astype(bf16)]
    all_to_all x1, waiting for transfers between devices: 0.01 us -> 2.02 us  [on_device(): terms = lax.all_to_all(terms, HEAD, 0, 0)]
    ppermute x7, waiting for transfers between devices: 18.2 us -> 16.2 us  [on_device(): lax.ppermute(part, 'z', [(i, (i + k) % n_z) for i in range(n_z)])]
    pallas_call x2 -> x3, Pallas kernels: 10.9 us -> 12.8 us  [the longest x1 11.7 us: attention_stats(): pl.pallas_call(stats_kernel, out_shape=(jax.ShapeDtypeStruct((3, 8, width...]
  transfers between devices with their start and end apart: 24 -> 24, of which waited for: 13 -> 13; matrix products, arithmetic and copies ran while one was open for 2% -> 2% of each run, Pallas kernels for 15% -> 18%
where the time goes in v2:
time: 146 us
  waiting for transfers between devices  48.8 us (33%)
  starting transfers between devices  47.5 us (33%)
  Pallas kernels  43.8 us (30%)
  local copies, waits for them, and re-layouts  3.64 us (2%)
    ppermute x7, waiting for transfers between devices, on_device(): lax.ppermute(part, 'z', [(i, (i + k) % n_z) for i in range(n_z)])  16.2 us
    pallas_call x1, Pallas kernels, attention_grads(): pl.pallas_call(grads_kernel, out_shape=(jax.ShapeDtypeStruct(shape, f32),...  13.6 us
    ppermute x11, waiting for transfers between devices, swap(): return lax.ppermute(x, axis, [(0, 1), (1, 0)])  12.3 us
    pallas_call x1, Pallas kernels, attention_stats(): pl.pallas_call(stats_kernel, out_shape=(jax.ShapeDtypeStruct((3, 8, width...  11.7 us
    ppermute x11, starting transfers between devices, swap(): return lax.ppermute(x, axis, [(0, 1), (1, 0)])  11.2 us
    ppermute x7, starting transfers between devices, on_device(): lax.ppermute(part, 'z', [(i, (i + k) % n_z) for i in range(n_z)])  9.54 us
    all_to_all x1, starting transfers between devices, on_device(): dkv = lax.all_to_all(dkv, 'z', 0, 0)  8.83 us
    all_to_all x1, starting transfers between devices, on_device(): packed = lax.all_to_all(packed, 'z', 0, 0)  8.47 us
  transfers between devices with their start and end apart: 24, of which 13 were waited for; matrix products, arithmetic and copies ran while one was open for 2% of the time, Pallas kernels for 18%

profile of v2, /device:TPU:24, one launch (start us, length us, event | category | flops | bytes accessed | tf_op | source)
XLA Modules:
  0.0 145.6 jit_solution(12045532472937059091)
XLA Ops:
  0.6 2.5 %gather.1 = (bf16[128,2048]{1,0:T(8,128)(2,1)}, bf16[8,128,256]{2,1,0:T(8,128)(2,1)}) custom-call(bf16[128,512]{1,0:T(8,128)(2,1)} %refs_0_.1, bf16[128,512]{1,0:T(8,128)(2,1)} %refs_1_.1, bf16[128,512]{1,0:T(8,128)(2,1)} %refs_2_.1, bf16[128,512]{1,0:T(8,128)(2,1)} %refs_3_.1, bf16[128,128]{1,0:T(8,128)(2,1)} %refs_4_.1, bf16[128,128]{1,0:T(8,128)(2,1)} %refs_5_.1), custom_call_target="tpu_custom_call" | custom-call | tf_op jit(solution)/shard_map/gather/pallas_call | solution.py:331
  3.1 3.1 %collective-permute-start = (bf16[128,2048]{1,0:T(8,128)(2,1)}, bf16[128,2048]{1,0:T(8,128)(2,1)S(1)}, u32[]{:S(2)}, u32[]{:S(2)}) collective-permute-start(bf16[128,2048]{1,0:T(8,128)(2,1)} %get-tuple-element.57.own), channel_id=1, source_target_pairs={{0,128},{128,0},{1,129},{129,1},{2,130},{130,2},{3,131},{131,3},{4... | collective-permute-start | bytes 1572872 | tf_op jit(solution)/shard_map/gather/ppermute | solution.py:491
  6.2 8.5 %all-to-all-start = ((bf16[8,128,256]{2,1,0:T(8,128)(2,1)}), bf16[8,128,256]{2,1,0:T(8,128)(2,1)S(1)}, u32[]{:S(2)}, u32[]{:S(2)}) async-start(bf16[8,128,256]{2,1,0:T(8,128)(2,1)} %get-tuple-element.54), calls=%async_computation | async-start | bytes 1048576 | tf_op jit(solution)/shard_map/gather/all_to_all | solution.py:523
  14.7 0.6 pad_add_fusion.at
  15.3 3.9 %spread_input.1 = (bf16[8,128,256]{2,1,0:T(8,128)(2,1)}, bf16[8,128,256]{2,1,0:T(8,128)(2,1)}, bf16[8,128,256]{2,1,0:T(8,128)(2,1)}, bf16[8,128,256]{2,1,0:T(8,128)(2,1)}) custom-call(s32[2]{0:T(128)} %pad_add_fusion.at, bf16[128,8192]{1,0:T(8,128)(2,1)} %x), custom_call_target="tpu_custom_call" | custom-call | tf_op jit(solution)/shard_map/spread_input/pallas_call | solution.py:360
  19.2 0.6 collective-permute-start.2
  19.8 1.8 %collective-permute-start.3 = (bf16[8,128,256]{2,1,0:T(8,128)(2,1)}, bf16[8,128,256]{2,1,0:T(8,128)(2,1)S(1)}, u32[]{:S(2)}, u32[]{:S(2)}) collective-permute-start(bf16[8,128,256]{2,1,0:T(8,128)(2,1)} %get-tuple-element.71), channel_id=1, source_target_pairs={{0,128},{128,0},{1,129},{129,1},{2,130},{130,2},{3,131},{131,3},{4... | collective-permute-start | bytes 1572872 | tf_op jit(solution)/shard_map/spread_input/ppermute | solution.py:491
  21.6 0.2 collective-permute-start.4
  21.9 1.6 %collective-permute-start.5 = (bf16[8,128,256]{2,1,0:T(8,128)(2,1)}, bf16[8,128,256]{2,1,0:T(8,128)(2,1)S(1)}, u32[]{:S(2)}, u32[]{:S(2)}) collective-permute-start(bf16[8,128,256]{2,1,0:T(8,128)(2,1)} %get-tuple-element.73), channel_id=1, source_target_pairs={{0,136},{8,128},{128,8},{136,0},{1,137},{9,129},{129,9},{137,1},{2... | collective-permute-start | bytes 1572872 | tf_op jit(solution)/shard_map/spread_input/ppermute | solution.py:495
  23.4 0.7 stack.60.where
  24.1 7.8 %all-to-all-done.kv = bf16[8,128,256]{2,1,0:T(8,128)(2,1)S(1)} async-done(((bf16[8,128,256]{2,1,0:T(8,128)(2,1)}), bf16[8,128,256]{2,1,0:T(8,128)(2,1)S(1)}, u32[]{:S(2)}, u32[]{:S(2)}) %all-to-all-start) | async-done | bytes 524320 | tf_op jit(solution)/shard_map/gather/all_to_all | solution.py:523
  31.9 0.0 collective-permute-done.1.side
  31.9 0.0 collective-permute-done.2.both
  32.0 0.8 copy-done.5
  32.7 0.2 copy-done.12
  32.9 11.7 %attention_stats.1 = (f32[3,8,512]{2,1,0:T(8,128)}, bf16[1024,128]{1,0:T(8,128)(2,1)}, bf16[1024,128]{1,0:T(8,128)(2,1)}, bf16[4,2,512,128]{3,2,1,0:T(8,128)(2,1)}, bf16[4,2,512,128]{3,2,1,0:T(8,128)(2,1)}) custom-call(s32[64]{0:T(128)} %order.3, s32[12]{0:T(128)} %stack.60.where, bf16[128,2048]{1,0:T(8,128)(2,1)} %get-tuple-element.57.own, ...), custom_call_target="tpu_custom_call" | custom-call | flops 1073741824 | bytes 8388608 | tf_op jit(solution)/shard_map/attention_stats/pallas_call | solution.py:271
  44.6 0.0 collective-permute-done.3.x1
  44.7 0.0 collective-permute-done.4.x2
  44.7 1.1 collective-permute-done.5.x3
  45.8 2.5 %collective-permute-start.8 = (f32[3,8,512]{2,1,0:T(8,128)}, f32[3,8,512]{2,1,0:T(8,128)S(1)}, u32[]{:S(2)}, u32[]{:S(2)}) collective-permute-start(f32[3,8,512]{2,1,0:T(8,128)} %get-tuple-element.74.s_own), channel_id=1, source_target_pairs={{0,136},{8,128},{128,8},{136,0},{1,137},{9,129},{129,9},{137,1},{2... | collective-permute-start | bytes 147464 | tf_op jit(solution)/shard_map/share_stats/ppermute | solution.py:495
  48.3 0.3 collective-permute-start.7
  48.6 1.0 collective-permute-start.6
  49.6 1.4 collective-permute-done.8.s_both
  51.1 0.0 collective-permute-done.7.s_side
  51.1 3.4 %collective-permute-done.6.s_far = f32[3,8,512]{2,1,0:T(8,128)S(1)} collective-permute-done((f32[3,8,512]{2,1,0:T(8,128)}, f32[3,8,512]{2,1,0:T(8,128)S(1)}, u32[]{:S(2)}, u32[]{:S(2)}) %collective-permute-start.6) | collective-permute-done | bytes 49184 | tf_op jit(solution)/shard_map/share_stats/ppermute | solution.py:491
  54.5 0.6 copy-done.15
  55.1 13.6 %attention_grads.1 = (f32[128,1024]{1,0:T(8,128)}, f32[128,1024]{1,0:T(8,128)}, bf16[2,128,1024]{2,1,0:T(8,128)(2,1)}, bf16[8,128,256]{2,1,0:T(8,128)(2,1)}) custom-call(s32[64]{0:T(128)} %order.3, s32[12]{0:T(128)} %stack.60.where, bf16[1024,128]{1,0:T(8,128)(2,1)} %get-tuple-element.65.keys, bf16[1024,128]{1,0:T(8,128)(2,1)} %get-tuple-element.66.values, ...), custom_call_target="tpu_custom_call" | custom-call | flops 2684354560 | bytes 8388608 | tf_op jit(solution)/shard_map/attention_grads/pallas_call | solution.py:290
  68.7 0.1 collective-permute-start.9
  68.8 8.8 %all-to-all-start.1 = ((bf16[8,128,256]{2,1,0:T(8,128)(2,1)}), bf16[8,128,256]{2,1,0:T(8,128)(2,1)S(1)}, u32[]{:S(2)}, u32[]{:S(2)}) async-start(bf16[8,128,256]{2,1,0:T(8,128)(2,1)} %get-tuple-element.75), calls=%async_computation.1 | async-start | bytes 1048576 | tf_op jit(solution)/shard_map/scatter_grads/all_to_all | solution.py:543
  77.6 0.1 convert_element_type.12
  77.7 0.2 fusion.1
  77.9 1.0 collective-permute-start.10
  78.9 8.9 %collective-permute-done.10 = bf16[128,1024]{1,0:T(8,128)(2,1)S(1)} collective-permute-done((bf16[128,1024]{1,0:T(8,128)(2,1)S(1)}, bf16[128,1024]{1,0:T(8,128)(2,1)S(1)}, u32[]{:S(2)}, u32[]{:S(2)}) %collective-permute-start.10) | collective-permute-done | bytes 262176 | tf_op jit(solution)/shard_map/query_grads/ppermute | solution.py:491
  87.8 7.8 %all-to-all-done.1.parts = bf16[8,128,256]{2,1,0:T(8,128)(2,1)S(1)} async-done(((bf16[8,128,256]{2,1,0:T(8,128)(2,1)}), bf16[8,128,256]{2,1,0:T(8,128)(2,1)S(1)}, u32[]{:S(2)}, u32[]{:S(2)}) %all-to-all-start.1) | async-done | bytes 524320 | tf_op jit(solution)/shard_map/scatter_grads/all_to_all | solution.py:543
  95.6 0.1 scatter_grads.1.grad.g0
  95.7 0.0 copy-start
  95.7 0.6 collective-permute-start.13
  96.3 0.5 collective-permute-start.12
  96.8 2.6 %collective-permute-start.11 = (bf16[128,256]{1,0:T(8,128)(2,1)S(1)}, bf16[128,256]{1,0:T(8,128)(2,1)S(1)}, u32[]{:S(2)}, u32[]{:S(2)}) collective-permute-start(bf16[128,256]{1,0:T(8,128)(2,1)S(1)} %scatter_grads.1.grad.g0), channel_id=1, source_target_pairs={{0,128},{128,0},{1,129},{129,1},{2,130},{130,2},{3,131},{131,3},{4... | collective-permute-start | bytes 196616 | tf_op jit(solution)/shard_map/scatter_grads/ppermute | solution.py:491
  99.4 5.8 %input_grad.2 = bf16[8,128,1024]{2,1,0:T(8,128)(2,1)} custom-call(bf16[128,256]{1,0:T(8,128)(2,1)} %copy-done, bf16[8192,128]{1,0:T(8,128)(2,1)} %key_weight.1, bf16[8192,128]{1,0:T(8,128)(2,1)} %value_weight.1), custom_call_target="tpu_custom_call" | custom-call | flops 536870912 | bytes 6291456 | tf_op jit(solution)/shard_map/input_grad/pallas_call | solution.py:410
  105.2 0.0 copy-start.9
  105.3 0.0 copy-start.10
  105.3 0.6 copy-done.8
  105.8 0.0 copy-done.9
  105.9 0.0 copy-done.10
  105.9 4.7 %all-to-all-start.2 = ((bf16[8,128,1024]{2,1,0:T(8,128)(2,1)}), bf16[8,128,1024]{2,1,0:T(8,128)(2,1)S(1)}, u32[]{:S(2)}, u32[]{:S(2)}) async-start(bf16[8,128,1024]{2,1,0:T(8,128)(2,1)} %input_grad.2), calls=%async_computation.2 | async-start | bytes 4194304 | tf_op jit(solution)/shard_map/input_grad/all_to_all | solution.py:561
  110.6 4.5 %weight_grad.2 = (f32[256,256]{1,0:T(8,128)}, bf16[256,256]{1,0:T(8,128)(2,1)}, bf16[256,256]{1,0:T(8,128)(2,1)}, bf16[256,256]{1,0:T(8,128)(2,1)}, bf16[256,256...) custom-call(s32[1]{0:T(128)} %bitcast.16.at, ...), custom_call_target="tpu_custom_call" | custom-call | flops 536870912 | bytes 4194304 | tf_op jit(solution)/shard_map/weight_grad/pallas_call | solution.py:453
  115.2 0.6 collective-permute-start.14
  115.8 0.1 add_convert_fusion
  115.9 2.8 %collective-permute-start.16 = (bf16[256,256]{1,0:T(8,128)(2,1)}, bf16[256,256]{1,0:T(8,128)(2,1)S(1)}, u32[]{:S(2)}, u32[]{:S(2)}) collective-permute-start(bf16[256,256]{1,0:T(8,128)(2,1)} %get-tuple-element.96), channel_id=1, source_target_pairs={{0,48},{16,64},{32,80},{48,96},{64,112},{80,0},{96,16},{112,32},{1... | collective-permute-start | bytes 393224 | tf_op jit(solution)/shard_map/weight_grad/ppermute | solution.py:568
  118.7 3.3 %collective-permute-start.17 = (bf16[256,256]{1,0:T(8,128)(2,1)}, bf16[256,256]{1,0:T(8,128)(2,1)S(1)}, u32[]{:S(2)}, u32[]{:S(2)}) collective-permute-start(bf16[256,256]{1,0:T(8,128)(2,1)} %get-tuple-element.97), channel_id=1, source_target_pairs={{0,64},{16,80},{32,96},{48,112},{64,0},{80,16},{96,32},{112,48},{1... | collective-permute-start | bytes 393224 | tf_op jit(solution)/shard_map/weight_grad/ppermute | solution.py:568
  122.0 1.3 collective-permute-start.18
  123.3 2.4 %collective-permute-done.14.refs_1_ = bf16[256,256]{1,0:T(8,128)(2,1)S(1)} collective-permute-done((bf16[256,256]{1,0:T(8,128)(2,1)}, bf16[256,256]{1,0:T(8,128)(2,1)S(1)}, u32[]{:S(2)}, u32[]{:S(2)}) %collective-permute-start.14) | collective-permute-done | bytes 131104 | tf_op jit(solution)/shard_map/weight_grad/ppermute | solution.py:568
  125.6 1.0 collective-permute-start.19
  126.6 5.4 %collective-permute-done.15.refs_2_ = bf16[256,256]{1,0:T(8,128)(2,1)S(1)} collective-permute-done((bf16[256,256]{1,0:T(8,128)(2,1)}, bf16[256,256]{1,0:T(8,128)(2,1)S(1)}, u32[]{:S(2)}, u32[]{:S(2)}) %collective-permute-start.15) | collective-permute-done | bytes 131104 | tf_op jit(solution)/shard_map/weight_grad/ppermute | solution.py:568
  132.0 0.5 collective-permute-start.20
  132.5 0.7 fusion.3
  133.2 2.0 %all-to-all-done.2.parts = bf16[8,128,1024]{2,1,0:T(8,128)(2,1)S(1)} async-done(((bf16[8,128,1024]{2,1,0:T(8,128)(2,1)}), bf16[8,128,1024]{2,1,0:T(8,128)(2,1)S(1)}, u32[]{:S(2)}, u32[]{:S(2)}) %all-to-all-start.2) | async-done | bytes 2097184 | tf_op jit(solution)/shard_map/input_grad/all_to_all | solution.py:561
  135.2 1.0 input_grad.3
  136.2 0.8 collective-permute-done.16.refs_3_
  137.0 0.4 collective-permute-done.18.refs_5_
  137.4 6.4 %collective-permute-done.19.refs_6_ = bf16[256,256]{1,0:T(8,128)(2,1)S(1)} collective-permute-done((bf16[256,256]{1,0:T(8,128)(2,1)}, bf16[256,256]{1,0:T(8,128)(2,1)S(1)}, u32[]{:S(2)}, u32[]{:S(2)}) %collective-permute-start.19) | collective-permute-done | bytes 131104 | tf_op jit(solution)/shard_map/weight_grad/ppermute | solution.py:568
  143.8 0.9 collective-permute-done.20.refs_7_
  144.7 0.8 weight_grad.3
  (31 shorter events, 0.1 us)
Async XLA Ops:
  3.1 16.1 %collective-permute-start = (bf16[128,2048]{1,0:T(8,128)(2,1)}, bf16[128,2048]{1,0:T(8,128)(2,1)S(1)}, u32[]{:S(2)}, u32[]{:S(2)}) collective-permute-start(bf16[128,2048]{1,0:T(8,128)(2,1)} %get-tuple-element.57.own), channel_id=1, source_target_pairs={{0,128},{128,0},{1,129},{129,1},{2,130},{130,2},{3,131},{131,3},{4... | collective-permute-start | bytes 1572872 | tf_op jit(solution)/shard_map/gather/ppermute | solution.py:491
  6.2 25.7 %all-to-all-start = ((bf16[8,128,256]{2,1,0:T(8,128)(2,1)}), bf16[8,128,256]{2,1,0:T(8,128)(2,1)S(1)}, u32[]{:S(2)}, u32[]{:S(2)}) async-start(bf16[8,128,256]{2,1,0:T(8,128)(2,1)} %get-tuple-element.54), calls=%async_computation | async-start | bytes 1048576 | tf_op jit(solution)/shard_map/gather/all_to_all | solution.py:523
  14.7 17.2 %collective-permute-start.1 = (bf16[128,2048]{1,0:T(8,128)(2,1)}, bf16[128,2048]{1,0:T(8,128)(2,1)S(1)}, u32[]{:S(2)}, u32[]{:S(2)}) collective-permute-start(bf16[128,2048]{1,0:T(8,128)(2,1)} %get-tuple-element.57.own), channel_id=1, source_target_pairs={{0,8},{8,0},{1,9},{9,1},{2,10},{10,2},{3,11},{11,3},{4,12},{12,4},... | collective-permute-start | bytes 1572872 | tf_op jit(solution)/shard_map/gather/ppermute | solution.py:491
  19.2 12.7 %copy-start.11 = (bf16[128,2048]{1,0:T(8,128)(2,1)}, bf16[128,2048]{1,0:T(8,128)(2,1)S(1)}, u32[]{:S(2)}) copy-start(bf16[128,2048]{1,0:T(8,128)(2,1)S(1)} %collective-permute-done.far) | copy-start | bytes 1572868
  19.2 12.7 %collective-permute-start.2 = (bf16[128,2048]{1,0:T(8,128)(2,1)S(1)}, bf16[128,2048]{1,0:T(8,128)(2,1)}, u32[]{:S(2)}, u32[]{:S(2)}) collective-permute-start(bf16[128,2048]{1,0:T(8,128)(2,1)S(1)} %collective-permute-done.far), channel_id=1, source_target_pairs={{0,8},{8,0},{1,9},{9,1},{2,10},{10,2},{3,11},{11,3},{4,12},{12,4},... | collective-permute-start | bytes 1572872 | tf_op jit(solution)/shard_map/spread_input/ppermute | solution.py:491
  19.8 24.8 %collective-permute-start.3 = (bf16[8,128,256]{2,1,0:T(8,128)(2,1)}, bf16[8,128,256]{2,1,0:T(8,128)(2,1)S(1)}, u32[]{:S(2)}, u32[]{:S(2)}) collective-permute-start(bf16[8,128,256]{2,1,0:T(8,128)(2,1)} %get-tuple-element.71), channel_id=1, source_target_pairs={{0,128},{128,0},{1,129},{129,1},{2,130},{130,2},{3,131},{131,3},{4... | collective-permute-start | bytes 1572872 | tf_op jit(solution)/shard_map/spread_input/ppermute | solution.py:491
  21.6 23.0 %collective-permute-start.4 = (bf16[8,128,256]{2,1,0:T(8,128)(2,1)}, bf16[8,128,256]{2,1,0:T(8,128)(2,1)S(1)}, u32[]{:S(2)}, u32[]{:S(2)}) collective-permute-start(bf16[8,128,256]{2,1,0:T(8,128)(2,1)} %get-tuple-element.72), channel_id=1, source_target_pairs={{0,8},{8,0},{1,9},{9,1},{2,10},{10,2},{3,11},{11,3},{4,12},{12,4},... | collective-permute-start | bytes 1572872 | tf_op jit(solution)/shard_map/spread_input/ppermute | solution.py:491
  21.9 24.0 %collective-permute-start.5 = (bf16[8,128,256]{2,1,0:T(8,128)(2,1)}, bf16[8,128,256]{2,1,0:T(8,128)(2,1)S(1)}, u32[]{:S(2)}, u32[]{:S(2)}) collective-permute-start(bf16[8,128,256]{2,1,0:T(8,128)(2,1)} %get-tuple-element.73), channel_id=1, source_target_pairs={{0,136},{8,128},{128,8},{136,0},{1,137},{9,129},{129,9},{137,1},{2... | collective-permute-start | bytes 1572872 | tf_op jit(solution)/shard_map/spread_input/ppermute | solution.py:495
  31.9 0.8 copy-start.5
  31.9 1.0 copy-start.12
  44.6 24.0 %copy-start.2 = (bf16[8,128,256]{2,1,0:T(8,128)(2,1)}, bf16[8,128,256]{2,1,0:T(8,128)(2,1)S(1)}, u32[]{:S(2)}) copy-start(bf16[8,128,256]{2,1,0:T(8,128)(2,1)S(1)} %collective-permute-done.3.x1) | copy-start | bytes 1572868
  44.7 24.0 %copy-start.3 = (bf16[8,128,256]{2,1,0:T(8,128)(2,1)}, bf16[8,128,256]{2,1,0:T(8,128)(2,1)S(1)}, u32[]{:S(2)}) copy-start(bf16[8,128,256]{2,1,0:T(8,128)(2,1)S(1)} %collective-permute-done.4.x2) | copy-start | bytes 1572868
  45.8 22.8 %copy-start.4 = (bf16[8,128,256]{2,1,0:T(8,128)(2,1)}, bf16[8,128,256]{2,1,0:T(8,128)(2,1)S(1)}, u32[]{:S(2)}) copy-start(bf16[8,128,256]{2,1,0:T(8,128)(2,1)S(1)} %collective-permute-done.5.x3) | copy-start | bytes 1572868
  45.8 5.2 %collective-permute-start.8 = (f32[3,8,512]{2,1,0:T(8,128)}, f32[3,8,512]{2,1,0:T(8,128)S(1)}, u32[]{:S(2)}, u32[]{:S(2)}) collective-permute-start(f32[3,8,512]{2,1,0:T(8,128)} %get-tuple-element.74.s_own), channel_id=1, source_target_pairs={{0,136},{8,128},{128,8},{136,0},{1,137},{9,129},{129,9},{137,1},{2... | collective-permute-start | bytes 147464 | tf_op jit(solution)/shard_map/share_stats/ppermute | solution.py:495
  48.3 2.7 %collective-permute-start.7 = (f32[3,8,512]{2,1,0:T(8,128)}, f32[3,8,512]{2,1,0:T(8,128)S(1)}, u32[]{:S(2)}, u32[]{:S(2)}) collective-permute-start(f32[3,8,512]{2,1,0:T(8,128)} %get-tuple-element.74.s_own), channel_id=1, source_target_pairs={{0,8},{8,0},{1,9},{9,1},{2,10},{10,2},{3,11},{11,3},{4,12},{12,4},... | collective-permute-start | bytes 147464 | tf_op jit(solution)/shard_map/share_stats/ppermute | solution.py:491
  48.6 5.8 %collective-permute-start.6 = (f32[3,8,512]{2,1,0:T(8,128)}, f32[3,8,512]{2,1,0:T(8,128)S(1)}, u32[]{:S(2)}, u32[]{:S(2)}) collective-permute-start(f32[3,8,512]{2,1,0:T(8,128)} %get-tuple-element.74.s_own), channel_id=1, source_target_pairs={{0,128},{128,0},{1,129},{129,1},{2,130},{130,2},{3,131},{131,3},{4... | collective-permute-start | bytes 147464 | tf_op jit(solution)/shard_map/share_stats/ppermute | solution.py:491
  51.1 3.4 %copy-start.13 = (f32[3,8,512]{2,1,0:T(8,128)}, f32[3,8,512]{2,1,0:T(8,128)S(1)}, u32[]{:S(2)}) copy-start(f32[3,8,512]{2,1,0:T(8,128)S(1)} %collective-permute-done.8.s_both) | copy-start | bytes 147460
  51.1 3.4 %copy-start.14 = (f32[3,8,512]{2,1,0:T(8,128)}, f32[3,8,512]{2,1,0:T(8,128)S(1)}, u32[]{:S(2)}) copy-start(f32[3,8,512]{2,1,0:T(8,128)S(1)} %collective-permute-done.7.s_side) | copy-start | bytes 147460
  54.5 0.6 copy-start.15
  68.7 9.1 %copy-start.6 = (f32[128,1024]{1,0:T(8,128)S(1)}, f32[128,1024]{1,0:T(8,128)}, u32[]{:S(2)}) copy-start(f32[128,1024]{1,0:T(8,128)} %get-tuple-element.76) | copy-start | bytes 1572868
  68.7 9.1 %copy-start.7 = (f32[128,1024]{1,0:T(8,128)S(1)}, f32[128,1024]{1,0:T(8,128)}, u32[]{:S(2)}) copy-start(f32[128,1024]{1,0:T(8,128)} %get-tuple-element.78) | copy-start | bytes 1572868
  68.7 8.9 %collective-permute-start.9 = (bf16[2,128,1024]{2,1,0:T(8,128)(2,1)}, bf16[2,128,1024]{2,1,0:T(8,128)(2,1)S(1)}, u32[]{:S(2)}, u32[]{:S(2)}) collective-permute-start(bf16[2,128,1024]{2,1,0:T(8,128)(2,1)} %get-tuple-element.77), channel_id=1, source_target_pairs={{0,8},{8,0},{1,9},{9,1},{2,10},{10,2},{3,11},{11,3},{4,12},{12,4},... | collective-permute-start | bytes 1572872 | tf_op jit(solution)/shard_map/query_grads/ppermute | solution.py:491
  68.8 26.8 %all-to-all-start.1 = ((bf16[8,128,256]{2,1,0:T(8,128)(2,1)}), bf16[8,128,256]{2,1,0:T(8,128)(2,1)S(1)}, u32[]{:S(2)}, u32[]{:S(2)}) async-start(bf16[8,128,256]{2,1,0:T(8,128)(2,1)} %get-tuple-element.75), calls=%async_computation.1 | async-start | bytes 1048576 | tf_op jit(solution)/shard_map/scatter_grads/all_to_all | solution.py:543
  77.9 9.9 %collective-permute-start.10 = (bf16[128,1024]{1,0:T(8,128)(2,1)S(1)}, bf16[128,1024]{1,0:T(8,128)(2,1)S(1)}, u32[]{:S(2)}, u32[]{:S(2)}) collective-permute-start(bf16[128,1024]{1,0:T(8,128)(2,1)S(1)} %get-tuple-element.103), channel_id=1, source_target_pairs={{0,128},{128,0},{1,129},{129,1},{2,130},{130,2},{3,131},{131,3},{4... | collective-permute-start | bytes 786440 | tf_op jit(solution)/shard_map/query_grads/ppermute | solution.py:491
  95.7 3.7 %copy-start = (bf16[128,256]{1,0:T(8,128)(2,1)}, bf16[128,256]{1,0:T(8,128)(2,1)S(1)}, u32[]{:S(2)}) copy-start(bf16[128,256]{1,0:T(8,128)(2,1)S(1)} %scatter_grads.1.grad.g0) | copy-start | bytes 196612
  95.7 9.5 %collective-permute-start.13 = (bf16[128,256]{1,0:T(8,128)(2,1)S(1)}, bf16[128,256]{1,0:T(8,128)(2,1)S(1)}, u32[]{:S(2)}, u32[]{:S(2)}) collective-permute-start(bf16[128,256]{1,0:T(8,128)(2,1)S(1)} %scatter_grads.1.grad.g0), channel_id=1, source_target_pairs={{0,136},{8,128},{128,8},{136,0},{1,137},{9,129},{129,9},{137,1},{2... | collective-permute-start | bytes 196616 | tf_op jit(solution)/shard_map/scatter_grads/ppermute | solution.py:495
  96.3 8.9 %collective-permute-start.12 = (bf16[128,256]{1,0:T(8,128)(2,1)S(1)}, bf16[128,256]{1,0:T(8,128)(2,1)S(1)}, u32[]{:S(2)}, u32[]{:S(2)}) collective-permute-start(bf16[128,256]{1,0:T(8,128)(2,1)S(1)} %scatter_grads.1.grad.g0), channel_id=1, source_target_pairs={{0,8},{8,0},{1,9},{9,1},{2,10},{10,2},{3,11},{11,3},{4,12},{12,4},... | collective-permute-start | bytes 196616 | tf_op jit(solution)/shard_map/scatter_grads/ppermute | solution.py:491
  96.8 8.5 %collective-permute-start.11 = (bf16[128,256]{1,0:T(8,128)(2,1)S(1)}, bf16[128,256]{1,0:T(8,128)(2,1)S(1)}, u32[]{:S(2)}, u32[]{:S(2)}) collective-permute-start(bf16[128,256]{1,0:T(8,128)(2,1)S(1)} %scatter_grads.1.grad.g0), channel_id=1, source_target_pairs={{0,128},{128,0},{1,129},{129,1},{2,130},{130,2},{3,131},{131,3},{4... | collective-permute-start | bytes 196616 | tf_op jit(solution)/shard_map/scatter_grads/ppermute | solution.py:491
  105.2 0.6 copy-start.8
  105.2 0.6 copy-start.9
  105.3 0.6 copy-start.10
  105.9 29.3 %all-to-all-start.2 = ((bf16[8,128,1024]{2,1,0:T(8,128)(2,1)}), bf16[8,128,1024]{2,1,0:T(8,128)(2,1)S(1)}, u32[]{:S(2)}, u32[]{:S(2)}) async-start(bf16[8,128,1024]{2,1,0:T(8,128)(2,1)} %input_grad.2), calls=%async_computation.2 | async-start | bytes 4194304 | tf_op jit(solution)/shard_map/input_grad/all_to_all | solution.py:561
  115.2 29.6 %copy-start.1 = (f32[256,256]{1,0:T(8,128)S(1)}, f32[256,256]{1,0:T(8,128)}, u32[]{:S(2)}) copy-start(f32[256,256]{1,0:T(8,128)} %get-tuple-element.93.refs_0_) | copy-start | bytes 786436
  115.2 10.4 %collective-permute-start.14 = (bf16[256,256]{1,0:T(8,128)(2,1)}, bf16[256,256]{1,0:T(8,128)(2,1)S(1)}, u32[]{:S(2)}, u32[]{:S(2)}) collective-permute-start(bf16[256,256]{1,0:T(8,128)(2,1)} %get-tuple-element.94), channel_id=1, source_target_pairs={{0,16},{16,32},{32,48},{48,64},{64,80},{80,96},{96,112},{112,0},{1... | collective-permute-start | bytes 393224 | tf_op jit(solution)/shard_map/weight_grad/ppermute | solution.py:568
  115.8 16.2 %collective-permute-start.15 = (bf16[256,256]{1,0:T(8,128)(2,1)}, bf16[256,256]{1,0:T(8,128)(2,1)S(1)}, u32[]{:S(2)}, u32[]{:S(2)}) collective-permute-start(bf16[256,256]{1,0:T(8,128)(2,1)} %get-tuple-element.95), channel_id=1, source_target_pairs={{0,32},{16,48},{32,64},{48,80},{64,96},{80,112},{96,0},{112,16},{1... | collective-permute-start | bytes 393224 | tf_op jit(solution)/shard_map/weight_grad/ppermute | solution.py:568
  115.9 21.1 %collective-permute-start.16 = (bf16[256,256]{1,0:T(8,128)(2,1)}, bf16[256,256]{1,0:T(8,128)(2,1)S(1)}, u32[]{:S(2)}, u32[]{:S(2)}) collective-permute-start(bf16[256,256]{1,0:T(8,128)(2,1)} %get-tuple-element.96), channel_id=1, source_target_pairs={{0,48},{16,64},{32,80},{48,96},{64,112},{80,0},{96,16},{112,32},{1... | collective-permute-start | bytes 393224 | tf_op jit(solution)/shard_map/weight_grad/ppermute | solution.py:568
  118.7 18.3 %collective-permute-start.17 = (bf16[256,256]{1,0:T(8,128)(2,1)}, bf16[256,256]{1,0:T(8,128)(2,1)S(1)}, u32[]{:S(2)}, u32[]{:S(2)}) collective-permute-start(bf16[256,256]{1,0:T(8,128)(2,1)} %get-tuple-element.97), channel_id=1, source_target_pairs={{0,64},{16,80},{32,96},{48,112},{64,0},{80,16},{96,32},{112,48},{1... | collective-permute-start | bytes 393224 | tf_op jit(solution)/shard_map/weight_grad/ppermute | solution.py:568
  122.0 15.5 %collective-permute-start.18 = (bf16[256,256]{1,0:T(8,128)(2,1)}, bf16[256,256]{1,0:T(8,128)(2,1)S(1)}, u32[]{:S(2)}, u32[]{:S(2)}) collective-permute-start(bf16[256,256]{1,0:T(8,128)(2,1)} %get-tuple-element.98), channel_id=1, source_target_pairs={{0,80},{16,96},{32,112},{48,0},{64,16},{80,32},{96,48},{112,64},{1... | collective-permute-start | bytes 393224 | tf_op jit(solution)/shard_map/weight_grad/ppermute | solution.py:568
  125.6 18.2 %collective-permute-start.19 = (bf16[256,256]{1,0:T(8,128)(2,1)}, bf16[256,256]{1,0:T(8,128)(2,1)S(1)}, u32[]{:S(2)}, u32[]{:S(2)}) collective-permute-start(bf16[256,256]{1,0:T(8,128)(2,1)} %get-tuple-element.99), channel_id=1, source_target_pairs={{0,96},{16,112},{32,0},{48,16},{64,32},{80,48},{96,64},{112,80},{1... | collective-permute-start | bytes 393224 | tf_op jit(solution)/shard_map/weight_grad/ppermute | solution.py:568
  132.0 12.8 %collective-permute-start.20 = (bf16[256,256]{1,0:T(8,128)(2,1)}, bf16[256,256]{1,0:T(8,128)(2,1)S(1)}, u32[]{:S(2)}, u32[]{:S(2)}) collective-permute-start(bf16[256,256]{1,0:T(8,128)(2,1)} %get-tuple-element.100), channel_id=1, source_target_pairs={{0,112},{16,0},{32,16},{48,32},{64,48},{80,64},{96,80},{112,96},{1... | collective-permute-start | bytes 393224 | tf_op jit(solution)/shard_map/weight_grad/ppermute | solution.py:568

commit v3 on v2

--- a/solution.py
+++ b/solution.py
@@ -460,7 +460,7 @@
             pltpu.VMEM((columns, 4 * rows), bf16),
             pltpu.SemaphoreType.DMA((4,)),
         ],
-        compiler_params=pltpu.CompilerParams(vmem_limit_bytes=BIG),
+        compiler_params=pltpu.CompilerParams(vmem_limit_bytes=14 * 2**20),
         cost_estimate=pl.CostEstimate(
             flops=8 * rows * n_z * shape[0] * shape[1], bytes_accessed=4 * 2**20, transcendentals=0
         ),
@@ -533,8 +533,9 @@
     with jax.named_scope("attention_stats"):
         stats, *sorted_rows = attention_stats(block_order, where, own, far, side, both, packed)
     with jax.named_scope("share_stats"):
+        others = [swap(stats, "xh"), swap(stats, "core"), cross(stats)]
         stats, *cuts = lax.optimization_barrier((stats, *cuts))
-        stats = (stats, swap(stats, "xh"), swap(stats, "core"), cross(stats))
+        stats = [stats] + others
     with jax.named_scope("attention_grads"):
         dq_own, dq_far, dq_pair, dkv = attention_grads(
             block_order, where, *sorted_rows, stats, n_z

time: 146 us -> 144 us (0.986)
  waiting for transfers between devices: 48.8 us -> 42.3 us
  local copies, waits for them, and re-layouts: 3.64 us -> 6.55 us
  other arithmetic: 0.91 us -> 2.63 us
    ppermute x11, waiting for transfers between devices: 12.3 us -> 7.91 us  [swap(): return lax.ppermute(x, axis, [(0, 1), (1, 0)])]
    all_to_all x1, starting transfers between devices: 8.83 us -> 4.84 us  [on_device(): dkv = lax.all_to_all(dkv, 'z', 0, 0)]
    ppermute x11, starting transfers between devices: 11.2 us -> 14.3 us  [swap(): return lax.ppermute(x, axis, [(0, 1), (1, 0)])]
    unnamed x32, local copies, waits for them, and re-layouts: 2.25 us -> 5.16 us
    pallas_call x1, Pallas kernels: 4.52 us -> 2.98 us  [weight_terms(): pl.pallas_call(weight_terms_kernel, out_shape=[jax.ShapeDtypeStruct(shape...]
  transfers between devices with their start and end apart: 24 -> 24, of which waited for: 13 -> 12; matrix products, arithmetic and copies ran while one was open for 2% -> 3% of each run, Pallas kernels for 18% -> 18%
where the time goes in v3:
time: 144 us; the launch traced here: 142 us
  starting transfers between devices  47.2 us (33%)
  Pallas kernels  42.9 us (30%)
  waiting for transfers between devices  42.3 us (29%)
  local copies, waits for them, and re-layouts  6.55 us (5%)
  other arithmetic  2.63 us (2%)
    ppermute x7, waiting for transfers between devices, on_device(): lax.ppermute(part, 'z', [(i, (i + k) % n_z) for i in range(n_z)])  17 us
    ppermute x11, starting transfers between devices, swap(): return lax.ppermute(x, axis, [(0, 1), (1, 0)])  14.3 us
    pallas_call x1, Pallas kernels, attention_grads(): pl.pallas_call(grads_kernel, out_shape=(jax.ShapeDtypeStruct(shape, f32),...  13.6 us
    pallas_call x1, Pallas kernels, attention_stats(): pl.pallas_call(stats_kernel, out_shape=(jax.ShapeDtypeStruct((3, 8, width...  11.7 us
    ppermute x7, starting transfers between devices, on_device(): lax.ppermute(part, 'z', [(i, (i + k) % n_z) for i in range(n_z)])  9.91 us
    all_to_all x1, starting transfers between devices, on_device(): packed = lax.all_to_all(packed, 'z', 0, 0)  8.47 us
    ppermute x11, waiting for transfers between devices, swap(): return lax.ppermute(x, axis, [(0, 1), (1, 0)])  7.91 us
    all_to_all x1, waiting for transfers between devices, on_device(): packed = lax.all_to_all(packed, 'z', 0, 0)  7.83 us
  transfers between devices with their start and end apart: 24, of which 12 were waited for; matrix products, arithmetic and copies ran while one was open for 3% of the time, Pallas kernels for 18%

profile of v3, /device:TPU:24, one launch (start us, length us, event | category | flops | bytes accessed | tf_op | source)
XLA Modules:
  0.0 142.5 jit_solution(5878196191050376266)
XLA Ops:
  0.6 2.5 %gather.1 = (bf16[128,2048]{1,0:T(8,128)(2,1)}, bf16[8,128,256]{2,1,0:T(8,128)(2,1)}) custom-call(bf16[128,512]{1,0:T(8,128)(2,1)} %refs_0_.1, bf16[128,512]{1,0:T(8,128)(2,1)} %refs_1_.1, bf16[128,512]{1,0:T(8,128)(2,1)} %refs_2_.1, bf16[128,512]{1,0:T(8,128)(2,1)} %refs_3_.1, bf16[128,128]{1,0:T(8,128)(2,1)} %refs_4_.1, bf16[128,128]{1,0:T(8,128)(2,1)} %refs_5_.1), custom_call_target="tpu_custom_call" | custom-call | tf_op jit(solution)/shard_map/gather/pallas_call | solution.py:331
  3.1 3.1 %collective-permute-start = (bf16[128,2048]{1,0:T(8,128)(2,1)}, bf16[128,2048]{1,0:T(8,128)(2,1)S(1)}, u32[]{:S(2)}, u32[]{:S(2)}) collective-permute-start(bf16[128,2048]{1,0:T(8,128)(2,1)} %get-tuple-element.57.own), channel_id=1, source_target_pairs={{0,128},{128,0},{1,129},{129,1},{2,130},{130,2},{3,131},{131,3},{4... | collective-permute-start | bytes 1572872 | tf_op jit(solution)/shard_map/gather/ppermute | solution.py:491
  6.2 8.5 %all-to-all-start = ((bf16[8,128,256]{2,1,0:T(8,128)(2,1)}), bf16[8,128,256]{2,1,0:T(8,128)(2,1)S(1)}, u32[]{:S(2)}, u32[]{:S(2)}) async-start(bf16[8,128,256]{2,1,0:T(8,128)(2,1)} %get-tuple-element.54), calls=%async_computation | async-start | bytes 1048576 | tf_op jit(solution)/shard_map/gather/all_to_all | solution.py:523
  14.7 0.0 collective-permute-start.1
  14.7 0.6 pad_add_fusion.at
  15.3 3.8 %spread_input.1 = (bf16[8,128,256]{2,1,0:T(8,128)(2,1)}, bf16[8,128,256]{2,1,0:T(8,128)(2,1)}, bf16[8,128,256]{2,1,0:T(8,128)(2,1)}, bf16[8,128,256]{2,1,0:T(8,128)(2,1)}) custom-call(s32[2]{0:T(128)} %pad_add_fusion.at, bf16[128,8192]{1,0:T(8,128)(2,1)} %x), custom_call_target="tpu_custom_call" | custom-call | tf_op jit(solution)/shard_map/spread_input/pallas_call | solution.py:360
  19.2 0.0 collective-permute-done.far
  19.2 0.6 collective-permute-start.2
  19.8 1.9 %collective-permute-start.3 = (bf16[8,128,256]{2,1,0:T(8,128)(2,1)}, bf16[8,128,256]{2,1,0:T(8,128)(2,1)S(1)}, u32[]{:S(2)}, u32[]{:S(2)}) collective-permute-start(bf16[8,128,256]{2,1,0:T(8,128)(2,1)} %get-tuple-element.71), channel_id=1, source_target_pairs={{0,128},{128,0},{1,129},{129,1},{2,130},{130,2},{3,131},{131,3},{4... | collective-permute-start | bytes 1572872 | tf_op jit(solution)/shard_map/spread_input/ppermute | solution.py:491
  21.6 0.2 collective-permute-start.4
  21.9 1.6 %collective-permute-start.5 = (bf16[8,128,256]{2,1,0:T(8,128)(2,1)}, bf16[8,128,256]{2,1,0:T(8,128)(2,1)S(1)}, u32[]{:S(2)}, u32[]{:S(2)}) collective-permute-start(bf16[8,128,256]{2,1,0:T(8,128)(2,1)} %get-tuple-element.73), channel_id=1, source_target_pairs={{0,136},{8,128},{128,8},{136,0},{1,137},{9,129},{129,9},{137,1},{2... | collective-permute-start | bytes 1572872 | tf_op jit(solution)/shard_map/spread_input/ppermute | solution.py:495
  23.4 0.7 stack.60.where
  24.1 7.8 %all-to-all-done.kv = bf16[8,128,256]{2,1,0:T(8,128)(2,1)S(1)} async-done(((bf16[8,128,256]{2,1,0:T(8,128)(2,1)}), bf16[8,128,256]{2,1,0:T(8,128)(2,1)S(1)}, u32[]{:S(2)}, u32[]{:S(2)}) %all-to-all-start) | async-done | bytes 524320 | tf_op jit(solution)/shard_map/gather/all_to_all | solution.py:523
  32.0 0.8 copy-done.8
  32.7 0.2 copy-done.12
  32.9 11.7 %attention_stats.1 = (f32[3,8,512]{2,1,0:T(8,128)}, bf16[1024,128]{1,0:T(8,128)(2,1)}, bf16[1024,128]{1,0:T(8,128)(2,1)}, bf16[4,2,512,128]{3,2,1,0:T(8,128)(2,1)}, bf16[4,2,512,128]{3,2,1,0:T(8,128)(2,1)}) custom-call(s32[64]{0:T(128)} %order.3, s32[12]{0:T(128)} %stack.60.where, bf16[128,2048]{1,0:T(8,128)(2,1)} %get-tuple-element.57.own, ...), custom_call_target="tpu_custom_call" | custom-call | flops 1073741824 | bytes 8388608 | tf_op jit(solution)/shard_map/attention_stats/pallas_call | solution.py:271
  44.6 0.3 collective-permute-start.8
  44.9 0.1 collective-permute-start.7
  45.1 3.5 %collective-permute-start.6 = (f32[3,8,512]{2,1,0:T(8,128)}, f32[3,8,512]{2,1,0:T(8,128)S(1)}, u32[]{:S(2)}, u32[]{:S(2)}) collective-permute-start(f32[3,8,512]{2,1,0:T(8,128)} %get-tuple-element.74.s_own), channel_id=1, source_target_pairs={{0,128},{128,0},{1,129},{129,1},{2,130},{130,2},{3,131},{131,3},{4... | collective-permute-start | bytes 147464 | tf_op jit(solution)/shard_map/share_stats/ppermute | solution.py:491
  48.6 0.0 collective-permute-done.4.x2
  48.6 0.0 collective-permute-done.5.x3
  48.6 1.6 %collective-permute-done.8.s_both = f32[3,8,512]{2,1,0:T(8,128)S(1)} collective-permute-done((f32[3,8,512]{2,1,0:T(8,128)}, f32[3,8,512]{2,1,0:T(8,128)S(1)}, u32[]{:S(2)}, u32[]{:S(2)}) %collective-permute-start.8) | collective-permute-done | bytes 49184 | tf_op jit(solution)/shard_map/share_stats/ppermute | solution.py:495
  50.1 1.0 collective-permute-done.6.s_far
  51.2 0.6 copy-done.15
  51.8 13.6 %attention_grads.1 = (f32[128,1024]{1,0:T(8,128)}, f32[128,1024]{1,0:T(8,128)}, bf16[2,128,1024]{2,1,0:T(8,128)(2,1)}, bf16[8,128,256]{2,1,0:T(8,128)(2,1)}) custom-call(s32[64]{0:T(128)} %order.3, s32[12]{0:T(128)} %stack.60.where, bf16[1024,128]{1,0:T(8,128)(2,1)} %get-tuple-element.65.keys, bf16[1024,128]{1,0:T(8,128)(2,1)} %get-tuple-element.66.values, ...), custom_call_target="tpu_custom_call" | custom-call | flops 2684354560 | bytes 8388608 | tf_op jit(solution)/shard_map/attention_grads/pallas_call | solution.py:290
  65.4 0.3 collective-permute-start.9
  65.7 4.8 %all-to-all-start.1 = ((bf16[8,128,256]{2,1,0:T(8,128)(2,1)}), bf16[8,128,256]{2,1,0:T(8,128)(2,1)S(1)}, u32[]{:S(2)}, u32[]{:S(2)}) async-start(bf16[8,128,256]{2,1,0:T(8,128)(2,1)} %get-tuple-element.75), calls=%async_computation.1 | async-start | bytes 1048576 | tf_op jit(solution)/shard_map/scatter_grads/all_to_all | solution.py:544
  70.6 0.0 collective-permute-done.9
  70.6 0.1 convert_element_type.12
  70.7 0.9 fusion.1
  71.7 3.2 %collective-permute-start.10 = (bf16[128,1024]{1,0:T(8,128)(2,1)S(1)}, bf16[128,1024]{1,0:T(8,128)(2,1)}, u32[]{:S(2)}, u32[]{:S(2)}) collective-permute-start(bf16[128,1024]{1,0:T(8,128)(2,1)S(1)} %get-tuple-element.103), channel_id=1, source_target_pairs={{0,128},{128,0},{1,129},{129,1},{2,130},{130,2},{3,131},{131,3},{4... | collective-permute-start | bytes 786440 | tf_op jit(solution)/shard_map/query_grads/ppermute | solution.py:491
  74.8 6.8 %collective-permute-done.10 = bf16[128,1024]{1,0:T(8,128)(2,1)} collective-permute-done((bf16[128,1024]{1,0:T(8,128)(2,1)S(1)}, bf16[128,1024]{1,0:T(8,128)(2,1)}, u32[]{:S(2)}, u32[]{:S(2)}) %collective-permute-start.10) | collective-permute-done | bytes 262176 | tf_op jit(solution)/shard_map/query_grads/ppermute | solution.py:491
  81.7 7.1 %all-to-all-done.1.parts = bf16[8,128,256]{2,1,0:T(8,128)(2,1)S(1)} async-done(((bf16[8,128,256]{2,1,0:T(8,128)(2,1)}), bf16[8,128,256]{2,1,0:T(8,128)(2,1)S(1)}, u32[]{:S(2)}, u32[]{:S(2)}) %all-to-all-start.1) | async-done | bytes 524320 | tf_op jit(solution)/shard_map/scatter_grads/all_to_all | solution.py:544
  88.8 0.7 scatter_grads.1.grad.g0
  89.5 2.3 %collective-permute-start.13 = (bf16[128,256]{1,0:T(8,128)(2,1)}, bf16[128,256]{1,0:T(8,128)(2,1)S(1)}, u32[]{:S(2)}, u32[]{:S(2)}) collective-permute-start(bf16[128,256]{1,0:T(8,128)(2,1)} %scatter_grads.1.grad.g0), channel_id=1, source_target_pairs={{0,136},{8,128},{128,8},{136,0},{1,137},{9,129},{129,9},{137,1},{2... | collective-permute-start | bytes 196616 | tf_op jit(solution)/shard_map/scatter_grads/ppermute | solution.py:495
  91.8 0.5 collective-permute-start.12
  92.3 0.9 collective-permute-start.11
  93.1 5.8 %input_grad.2 = bf16[8,128,1024]{2,1,0:T(8,128)(2,1)} custom-call(bf16[128,256]{1,0:T(8,128)(2,1)} %scatter_grads.1.grad.g0, bf16[8192,128]{1,0:T(8,128)(2,1)} %key_weight.1, bf16[8192,128]{1,0:T(8,128)(2,1)} %value_weight.1), custom_call_target="tpu_custom_call" | custom-call | flops 536870912 | bytes 6291456 | tf_op jit(solution)/shard_map/input_grad/pallas_call | solution.py:410
  99.0 0.0 collective-permute-done.11.g1
  99.0 0.0 copy-start.5
  99.0 0.6 copy-done.5
  99.6 5.6 %all-to-all-start.2 = ((bf16[8,128,1024]{2,1,0:T(8,128)(2,1)}), bf16[8,128,1024]{2,1,0:T(8,128)(2,1)S(1)}, u32[]{:S(2)}, u32[]{:S(2)}) async-start(bf16[8,128,1024]{2,1,0:T(8,128)(2,1)} %input_grad.2), calls=%async_computation.2 | async-start | bytes 4194304 | tf_op jit(solution)/shard_map/input_grad/all_to_all | solution.py:562
  105.2 1.0 copy-done.2
  106.3 1.0 copy-done.4
  107.3 0.8 copy-done.6
  108.1 3.0 %weight_grad.2 = (f32[256,256]{1,0:T(8,128)S(1)}, bf16[256,256]{1,0:T(8,128)(2,1)S(1)}, bf16[256,256]{1,0:T(8,128)(2,1)S(1)}, bf16[256,256]{1,0:T(8,128)(2,1)}, ...) custom-call(s32[1]{0:T(128)} %bitcast.16.at, ...), custom_call_target="tpu_custom_call" | custom-call | flops 536870912 | bytes 4194304 | tf_op jit(solution)/shard_map/weight_grad/pallas_call | solution.py:453
  111.1 0.6 collective-permute-start.14
  111.7 0.0 collective-permute-start.15
  111.7 1.0 add_convert_fusion
  112.7 2.8 %collective-permute-start.16 = (bf16[256,256]{1,0:T(8,128)(2,1)}, bf16[256,256]{1,0:T(8,128)(2,1)S(1)}, u32[]{:S(2)}, u32[]{:S(2)}) collective-permute-start(bf16[256,256]{1,0:T(8,128)(2,1)} %get-tuple-element.96), channel_id=1, source_target_pairs={{0,48},{16,64},{32,80},{48,96},{64,112},{80,0},{96,16},{112,32},{1... | collective-permute-start | bytes 393224 | tf_op jit(solution)/shard_map/weight_grad/ppermute | solution.py:569
  115.6 3.3 %collective-permute-start.17 = (bf16[256,256]{1,0:T(8,128)(2,1)}, bf16[256,256]{1,0:T(8,128)(2,1)S(1)}, u32[]{:S(2)}, u32[]{:S(2)}) collective-permute-start(bf16[256,256]{1,0:T(8,128)(2,1)} %get-tuple-element.97), channel_id=1, source_target_pairs={{0,64},{16,80},{32,96},{48,112},{64,0},{80,16},{96,32},{112,48},{1... | collective-permute-start | bytes 393224 | tf_op jit(solution)/shard_map/weight_grad/ppermute | solution.py:569
  118.8 1.3 collective-permute-start.18
  120.1 1.4 collective-permute-done.14.refs_1_
  121.6 1.9 %collective-permute-start.19 = (bf16[256,256]{1,0:T(8,128)(2,1)}, bf16[256,256]{1,0:T(8,128)(2,1)S(1)}, u32[]{:S(2)}, u32[]{:S(2)}) collective-permute-start(bf16[256,256]{1,0:T(8,128)(2,1)} %get-tuple-element.99), channel_id=1, source_target_pairs={{0,96},{16,112},{32,0},{48,16},{64,32},{80,48},{96,64},{112,80},{1... | collective-permute-start | bytes 393224 | tf_op jit(solution)/shard_map/weight_grad/ppermute | solution.py:569
  123.5 4.8 %collective-permute-done.15.refs_2_ = bf16[256,256]{1,0:T(8,128)(2,1)S(1)} collective-permute-done((bf16[256,256]{1,0:T(8,128)(2,1)S(1)}, bf16[256,256]{1,0:T(8,128)(2,1)S(1)}, u32[]{:S(2)}, u32[]{:S(2)}) %collective-permute-start.15) | collective-permute-done | bytes 131104 | tf_op jit(solution)/shard_map/weight_grad/ppermute | solution.py:569
  128.3 0.7 fusion.3
  129.0 0.9 all-to-all-done.2.parts
  129.8 1.0 input_grad.3
  130.8 1.9 %collective-permute-done.16.refs_3_ = bf16[256,256]{1,0:T(8,128)(2,1)S(1)} collective-permute-done((bf16[256,256]{1,0:T(8,128)(2,1)}, bf16[256,256]{1,0:T(8,128)(2,1)S(1)}, u32[]{:S(2)}, u32[]{:S(2)}) %collective-permute-start.16) | collective-permute-done | bytes 131104 | tf_op jit(solution)/shard_map/weight_grad/ppermute | solution.py:569
  132.7 0.0 collective-permute-done.17.refs_4_
  132.7 1.6 %collective-permute-done.18.refs_5_ = bf16[256,256]{1,0:T(8,128)(2,1)S(1)} collective-permute-done((bf16[256,256]{1,0:T(8,128)(2,1)}, bf16[256,256]{1,0:T(8,128)(2,1)S(1)}, u32[]{:S(2)}, u32[]{:S(2)}) %collective-permute-start.18) | collective-permute-done | bytes 131104 | tf_op jit(solution)/shard_map/weight_grad/ppermute | solution.py:569
  134.3 6.4 %collective-permute-done.19.refs_6_ = bf16[256,256]{1,0:T(8,128)(2,1)S(1)} collective-permute-done((bf16[256,256]{1,0:T(8,128)(2,1)}, bf16[256,256]{1,0:T(8,128)(2,1)S(1)}, u32[]{:S(2)}, u32[]{:S(2)}) %collective-permute-start.19) | collective-permute-done | bytes 131104 | tf_op jit(solution)/shard_map/weight_grad/ppermute | solution.py:569
  140.7 0.9 collective-permute-done.20.refs_7_
  141.6 0.8 weight_grad.3
  (31 shorter events, 0.1 us)
Async XLA Ops:
  3.1 16.0 %collective-permute-start = (bf16[128,2048]{1,0:T(8,128)(2,1)}, bf16[128,2048]{1,0:T(8,128)(2,1)S(1)}, u32[]{:S(2)}, u32[]{:S(2)}) collective-permute-start(bf16[128,2048]{1,0:T(8,128)(2,1)} %get-tuple-element.57.own), channel_id=1, source_target_pairs={{0,128},{128,0},{1,129},{129,1},{2,130},{130,2},{3,131},{131,3},{4... | collective-permute-start | bytes 1572872 | tf_op jit(solution)/shard_map/gather/ppermute | solution.py:491
  6.2 25.7 %all-to-all-start = ((bf16[8,128,256]{2,1,0:T(8,128)(2,1)}), bf16[8,128,256]{2,1,0:T(8,128)(2,1)S(1)}, u32[]{:S(2)}, u32[]{:S(2)}) async-start(bf16[8,128,256]{2,1,0:T(8,128)(2,1)} %get-tuple-element.54), calls=%async_computation | async-start | bytes 1048576 | tf_op jit(solution)/shard_map/gather/all_to_all | solution.py:523
  14.7 17.2 %collective-permute-start.1 = (bf16[128,2048]{1,0:T(8,128)(2,1)}, bf16[128,2048]{1,0:T(8,128)(2,1)S(1)}, u32[]{:S(2)}, u32[]{:S(2)}) collective-permute-start(bf16[128,2048]{1,0:T(8,128)(2,1)} %get-tuple-element.57.own), channel_id=1, source_target_pairs={{0,8},{8,0},{1,9},{9,1},{2,10},{10,2},{3,11},{11,3},{4,12},{12,4},... | collective-permute-start | bytes 1572872 | tf_op jit(solution)/shard_map/gather/ppermute | solution.py:491
  19.2 12.8 %copy-start.11 = (bf16[128,2048]{1,0:T(8,128)(2,1)}, bf16[128,2048]{1,0:T(8,128)(2,1)S(1)}, u32[]{:S(2)}) copy-start(bf16[128,2048]{1,0:T(8,128)(2,1)S(1)} %collective-permute-done.far) | copy-start | bytes 1572868
  19.2 12.7 %collective-permute-start.2 = (bf16[128,2048]{1,0:T(8,128)(2,1)S(1)}, bf16[128,2048]{1,0:T(8,128)(2,1)}, u32[]{:S(2)}, u32[]{:S(2)}) collective-permute-start(bf16[128,2048]{1,0:T(8,128)(2,1)S(1)} %collective-permute-done.far), channel_id=1, source_target_pairs={{0,8},{8,0},{1,9},{9,1},{2,10},{10,2},{3,11},{11,3},{4,12},{12,4},... | collective-permute-start | bytes 1572872 | tf_op jit(solution)/shard_map/spread_input/ppermute | solution.py:491
  19.8 25.3 %collective-permute-start.3 = (bf16[8,128,256]{2,1,0:T(8,128)(2,1)}, bf16[8,128,256]{2,1,0:T(8,128)(2,1)S(1)}, u32[]{:S(2)}, u32[]{:S(2)}) collective-permute-start(bf16[8,128,256]{2,1,0:T(8,128)(2,1)} %get-tuple-element.71), channel_id=1, source_target_pairs={{0,128},{128,0},{1,129},{129,1},{2,130},{130,2},{3,131},{131,3},{4... | collective-permute-start | bytes 1572872 | tf_op jit(solution)/shard_map/spread_input/ppermute | solution.py:491
  21.6 26.9 %collective-permute-start.4 = (bf16[8,128,256]{2,1,0:T(8,128)(2,1)}, bf16[8,128,256]{2,1,0:T(8,128)(2,1)S(1)}, u32[]{:S(2)}, u32[]{:S(2)}) collective-permute-start(bf16[8,128,256]{2,1,0:T(8,128)(2,1)} %get-tuple-element.72), channel_id=1, source_target_pairs={{0,8},{8,0},{1,9},{9,1},{2,10},{10,2},{3,11},{11,3},{4,12},{12,4},... | collective-permute-start | bytes 1572872 | tf_op jit(solution)/shard_map/spread_input/ppermute | solution.py:491
  21.9 26.7 %collective-permute-start.5 = (bf16[8,128,256]{2,1,0:T(8,128)(2,1)}, bf16[8,128,256]{2,1,0:T(8,128)(2,1)S(1)}, u32[]{:S(2)}, u32[]{:S(2)}) collective-permute-start(bf16[8,128,256]{2,1,0:T(8,128)(2,1)} %get-tuple-element.73), channel_id=1, source_target_pairs={{0,136},{8,128},{128,8},{136,0},{1,137},{9,129},{129,9},{137,1},{2... | collective-permute-start | bytes 1572872 | tf_op jit(solution)/shard_map/spread_input/ppermute | solution.py:495
  31.9 0.8 copy-start.8
  31.9 1.0 copy-start.12
  44.6 5.5 %collective-permute-start.8 = (f32[3,8,512]{2,1,0:T(8,128)}, f32[3,8,512]{2,1,0:T(8,128)S(1)}, u32[]{:S(2)}, u32[]{:S(2)}) collective-permute-start(f32[3,8,512]{2,1,0:T(8,128)} %get-tuple-element.74.s_own), channel_id=1, source_target_pairs={{0,136},{8,128},{128,8},{136,0},{1,137},{9,129},{129,9},{137,1},{2... | collective-permute-start | bytes 147464 | tf_op jit(solution)/shard_map/share_stats/ppermute | solution.py:495
  44.9 5.2 %collective-permute-start.7 = (f32[3,8,512]{2,1,0:T(8,128)}, f32[3,8,512]{2,1,0:T(8,128)S(1)}, u32[]{:S(2)}, u32[]{:S(2)}) collective-permute-start(f32[3,8,512]{2,1,0:T(8,128)} %get-tuple-element.74.s_own), channel_id=1, source_target_pairs={{0,8},{8,0},{1,9},{9,1},{2,10},{10,2},{3,11},{11,3},{4,12},{12,4},... | collective-permute-start | bytes 147464 | tf_op jit(solution)/shard_map/share_stats/ppermute | solution.py:491
  45.1 6.1 %collective-permute-start.6 = (f32[3,8,512]{2,1,0:T(8,128)}, f32[3,8,512]{2,1,0:T(8,128)S(1)}, u32[]{:S(2)}, u32[]{:S(2)}) collective-permute-start(f32[3,8,512]{2,1,0:T(8,128)} %get-tuple-element.74.s_own), channel_id=1, source_target_pairs={{0,128},{128,0},{1,129},{129,1},{2,130},{130,2},{3,131},{131,3},{4... | collective-permute-start | bytes 147464 | tf_op jit(solution)/shard_map/share_stats/ppermute | solution.py:491
  48.6 16.8 %copy-start.1 = (bf16[8,128,256]{2,1,0:T(8,128)(2,1)}, bf16[8,128,256]{2,1,0:T(8,128)(2,1)S(1)}, u32[]{:S(2)}) copy-start(bf16[8,128,256]{2,1,0:T(8,128)(2,1)S(1)} %collective-permute-done.4.x2) | copy-start | bytes 1572868
  48.6 16.8 %copy-start.3 = (bf16[8,128,256]{2,1,0:T(8,128)(2,1)}, bf16[8,128,256]{2,1,0:T(8,128)(2,1)S(1)}, u32[]{:S(2)}) copy-start(bf16[8,128,256]{2,1,0:T(8,128)(2,1)S(1)} %collective-permute-done.5.x3) | copy-start | bytes 1572868
  50.1 1.1 copy-start.13
  50.1 1.1 copy-start.14
  51.2 0.6 copy-start.15
  65.4 5.3 %copy-start.9 = (f32[128,1024]{1,0:T(8,128)S(1)}, f32[128,1024]{1,0:T(8,128)}, u32[]{:S(2)}) copy-start(f32[128,1024]{1,0:T(8,128)} %get-tuple-element.76) | copy-start | bytes 1572868
  65.4 5.3 %copy-start.10 = (f32[128,1024]{1,0:T(8,128)S(1)}, f32[128,1024]{1,0:T(8,128)}, u32[]{:S(2)}) copy-start(f32[128,1024]{1,0:T(8,128)} %get-tuple-element.78) | copy-start | bytes 1572868
  65.4 5.2 %collective-permute-start.9 = (bf16[2,128,1024]{2,1,0:T(8,128)(2,1)}, bf16[2,128,1024]{2,1,0:T(8,128)(2,1)S(1)}, u32[]{:S(2)}, u32[]{:S(2)}) collective-permute-start(bf16[2,128,1024]{2,1,0:T(8,128)(2,1)} %get-tuple-element.77), channel_id=1, source_target_pairs={{0,8},{8,0},{1,9},{9,1},{2,10},{10,2},{3,11},{11,3},{4,12},{12,4},... | collective-permute-start | bytes 1572872 | tf_op jit(solution)/shard_map/query_grads/ppermute | solution.py:491
  65.7 23.0 %all-to-all-start.1 = ((bf16[8,128,256]{2,1,0:T(8,128)(2,1)}), bf16[8,128,256]{2,1,0:T(8,128)(2,1)S(1)}, u32[]{:S(2)}, u32[]{:S(2)}) async-start(bf16[8,128,256]{2,1,0:T(8,128)(2,1)} %get-tuple-element.75), calls=%async_computation.1 | async-start | bytes 1048576 | tf_op jit(solution)/shard_map/scatter_grads/all_to_all | solution.py:544
  71.7 10.0 %collective-permute-start.10 = (bf16[128,1024]{1,0:T(8,128)(2,1)S(1)}, bf16[128,1024]{1,0:T(8,128)(2,1)}, u32[]{:S(2)}, u32[]{:S(2)}) collective-permute-start(bf16[128,1024]{1,0:T(8,128)(2,1)S(1)} %get-tuple-element.103), channel_id=1, source_target_pairs={{0,128},{128,0},{1,129},{129,1},{2,130},{130,2},{3,131},{131,3},{4... | collective-permute-start | bytes 786440 | tf_op jit(solution)/shard_map/query_grads/ppermute | solution.py:491
  89.5 9.5 %collective-permute-start.13 = (bf16[128,256]{1,0:T(8,128)(2,1)}, bf16[128,256]{1,0:T(8,128)(2,1)S(1)}, u32[]{:S(2)}, u32[]{:S(2)}) collective-permute-start(bf16[128,256]{1,0:T(8,128)(2,1)} %scatter_grads.1.grad.g0), channel_id=1, source_target_pairs={{0,136},{8,128},{128,8},{136,0},{1,137},{9,129},{129,9},{137,1},{2... | collective-permute-start | bytes 196616 | tf_op jit(solution)/shard_map/scatter_grads/ppermute | solution.py:495
  91.8 7.2 %collective-permute-start.12 = (bf16[128,256]{1,0:T(8,128)(2,1)}, bf16[128,256]{1,0:T(8,128)(2,1)S(1)}, u32[]{:S(2)}, u32[]{:S(2)}) collective-permute-start(bf16[128,256]{1,0:T(8,128)(2,1)} %scatter_grads.1.grad.g0), channel_id=1, source_target_pairs={{0,8},{8,0},{1,9},{9,1},{2,10},{10,2},{3,11},{11,3},{4,12},{12,4},... | collective-permute-start | bytes 196616 | tf_op jit(solution)/shard_map/scatter_grads/ppermute | solution.py:491
  92.3 6.7 %collective-permute-start.11 = (bf16[128,256]{1,0:T(8,128)(2,1)}, bf16[128,256]{1,0:T(8,128)(2,1)S(1)}, u32[]{:S(2)}, u32[]{:S(2)}) collective-permute-start(bf16[128,256]{1,0:T(8,128)(2,1)} %scatter_grads.1.grad.g0), channel_id=1, source_target_pairs={{0,128},{128,0},{1,129},{129,1},{2,130},{130,2},{3,131},{131,3},{4... | collective-permute-start | bytes 196616 | tf_op jit(solution)/shard_map/scatter_grads/ppermute | solution.py:491
  98.9 6.3 %copy-start = (bf16[8,128,256]{2,1,0:T(8,128)(2,1)S(1)}, bf16[8,128,256]{2,1,0:T(8,128)(2,1)}, u32[]{:S(2)}) copy-start(bf16[8,128,256]{2,1,0:T(8,128)(2,1)} %get-tuple-element.86.x0) | copy-start | bytes 1572868
  99.0 0.6 copy-start.5
  99.6 30.3 %all-to-all-start.2 = ((bf16[8,128,1024]{2,1,0:T(8,128)(2,1)}), bf16[8,128,1024]{2,1,0:T(8,128)(2,1)S(1)}, u32[]{:S(2)}, u32[]{:S(2)}) async-start(bf16[8,128,1024]{2,1,0:T(8,128)(2,1)} %input_grad.2), calls=%async_computation.2 | async-start | bytes 4194304 | tf_op jit(solution)/shard_map/input_grad/all_to_all | solution.py:562
  105.2 1.0 copy-start.2
  106.3 1.0 copy-start.4
  107.3 0.8 copy-start.6
  108.1 3.6 %copy-start.7 = (f32[128,1024]{1,0:T(8,128)S(1)}, f32[128,1024]{1,0:T(8,128)}, u32[]{:S(2)}) copy-start(f32[128,1024]{1,0:T(8,128)} %get-tuple-element.79) | copy-start | bytes 1572868
  111.1 10.4 %collective-permute-start.14 = (bf16[256,256]{1,0:T(8,128)(2,1)S(1)}, bf16[256,256]{1,0:T(8,128)(2,1)S(1)}, u32[]{:S(2)}, u32[]{:S(2)}) collective-permute-start(bf16[256,256]{1,0:T(8,128)(2,1)S(1)} %get-tuple-element.94), channel_id=1, source_target_pairs={{0,16},{16,32},{32,48},{48,64},{64,80},{80,96},{96,112},{112,0},{1... | collective-permute-start | bytes 393224 | tf_op jit(solution)/shard_map/weight_grad/ppermute | solution.py:569
  111.7 16.5 %collective-permute-start.15 = (bf16[256,256]{1,0:T(8,128)(2,1)S(1)}, bf16[256,256]{1,0:T(8,128)(2,1)S(1)}, u32[]{:S(2)}, u32[]{:S(2)}) collective-permute-start(bf16[256,256]{1,0:T(8,128)(2,1)S(1)} %get-tuple-element.95), channel_id=1, source_target_pairs={{0,32},{16,48},{32,64},{48,80},{64,96},{80,112},{96,0},{112,16},{1... | collective-permute-start | bytes 393224 | tf_op jit(solution)/shard_map/weight_grad/ppermute | solution.py:569
  112.7 19.9 %collective-permute-start.16 = (bf16[256,256]{1,0:T(8,128)(2,1)}, bf16[256,256]{1,0:T(8,128)(2,1)S(1)}, u32[]{:S(2)}, u32[]{:S(2)}) collective-permute-start(bf16[256,256]{1,0:T(8,128)(2,1)} %get-tuple-element.96), channel_id=1, source_target_pairs={{0,48},{16,64},{32,80},{48,96},{64,112},{80,0},{96,16},{112,32},{1... | collective-permute-start | bytes 393224 | tf_op jit(solution)/shard_map/weight_grad/ppermute | solution.py:569
  115.6 17.1 %collective-permute-start.17 = (bf16[256,256]{1,0:T(8,128)(2,1)}, bf16[256,256]{1,0:T(8,128)(2,1)S(1)}, u32[]{:S(2)}, u32[]{:S(2)}) collective-permute-start(bf16[256,256]{1,0:T(8,128)(2,1)} %get-tuple-element.97), channel_id=1, source_target_pairs={{0,64},{16,80},{32,96},{48,112},{64,0},{80,16},{96,32},{112,48},{1... | collective-permute-start | bytes 393224 | tf_op jit(solution)/shard_map/weight_grad/ppermute | solution.py:569
  118.8 15.5 %collective-permute-start.18 = (bf16[256,256]{1,0:T(8,128)(2,1)}, bf16[256,256]{1,0:T(8,128)(2,1)S(1)}, u32[]{:S(2)}, u32[]{:S(2)}) collective-permute-start(bf16[256,256]{1,0:T(8,128)(2,1)} %get-tuple-element.98), channel_id=1, source_target_pairs={{0,80},{16,96},{32,112},{48,0},{64,16},{80,32},{96,48},{112,64},{1... | collective-permute-start | bytes 393224 | tf_op jit(solution)/shard_map/weight_grad/ppermute | solution.py:569
  121.6 19.1 %collective-permute-start.19 = (bf16[256,256]{1,0:T(8,128)(2,1)}, bf16[256,256]{1,0:T(8,128)(2,1)S(1)}, u32[]{:S(2)}, u32[]{:S(2)}) collective-permute-start(bf16[256,256]{1,0:T(8,128)(2,1)} %get-tuple-element.99), channel_id=1, source_target_pairs={{0,96},{16,112},{32,0},{48,16},{64,32},{80,48},{96,64},{112,80},{1... | collective-permute-start | bytes 393224 | tf_op jit(solution)/shard_map/weight_grad/ppermute | solution.py:569
  128.3 13.4 %collective-permute-start.20 = (bf16[256,256]{1,0:T(8,128)(2,1)}, bf16[256,256]{1,0:T(8,128)(2,1)S(1)}, u32[]{:S(2)}, u32[]{:S(2)}) collective-permute-start(bf16[256,256]{1,0:T(8,128)(2,1)} %get-tuple-element.100), channel_id=1, source_target_pairs={{0,112},{16,0},{32,16},{48,32},{64,48},{80,64},{96,80},{112,96},{1... | collective-permute-start | bytes 393224 | tf_op jit(solution)/shard_map/weight_grad/ppermute | solution.py:569
